TPU v7x, 32 devices: a whole 2x2x4 slice. The times are simulated.
32 devices in a mesh: lat: 4 (over z), lon: 4 (over x, core), rep: 2 (over y).
Axes of the slice: x: 2, y: 2, z: 4, core: 2. Of those that a mesh axis runs over, the one named last changes fastest.
Arguments:
- latent: bfloat16 [6, 24, 384, 512], P('rep', 'lat', 'lon'), parts along dimension 0, may hold values from -6 to 6
- band_labels: int32 [24], replicated, may hold values from 0 to 5, never falling along the last dimension, each value on 1 to 8 neighbouring positions
- gain_first: float32 [512], replicated, may hold values from 0.1 to 1.9
- qkv_first: bfloat16 [512, 1536], replicated, may hold values from -2 to 2
- proj_first: bfloat16 [512, 512], replicated, may hold values from -1 to 1
- merge_gain: float32 [2048], replicated, may hold values from 0.1 to 1.9
- merge_weight: bfloat16 [2048, 1024], replicated, may hold values from -0.125 to 0.125
- gain_coarse: float32 [1024], replicated, may hold values from 0.1 to 1.9
- qkv_coarse: bfloat16 [1024, 3072], replicated, may hold values from -2 to 2
- proj_coarse: bfloat16 [1024, 1024], replicated, may hold values from -0.75 to 0.75
- split_gain: float32 [1024], replicated, may hold values from 0.1 to 1.9
- split_weight: bfloat16 [1024, 2048], replicated, may hold values from -0.1875 to 0.1875
- gain_last: float32 [512], replicated, may hold values from 0.1 to 1.9
- qkv_last: bfloat16 [512, 1536], replicated, may hold values from -2 to 2
- proj_last: bfloat16 [512, 512], replicated, may hold values from -1 to 1
Outputs:
- forecast_latent: bfloat16 [6, 24, 384, 512], P('rep', 'lat', 'lon'), parts along dimension 0
There are 2 independent parts, one for each index of `rep`. A program takes and returns all parts, laid end to end along the dimension named above; an argument that names none is the same for every part. Nothing has to cross between parts.
Inputs may be any that keep to these rules, and one draw needn't show every extreme that they name: `band_labels`: labels never fall along the rows, and each label covers 1 to 8 consecutive rows.
All inputs are finite; a program needn't handle non-finite values.
Results may differ from a plain program's by a relative error of at most 0.015.
Values may be sent and summed in bfloat16 or wider, within the bound.
No kernel may reach another device: no remote copies, remote signals or barrier semaphores. Data moves between devices by JAX's collectives and lax.ppermute only.
A program may use at most 128 MiB of HBM per device.

v0:
```python
import jax
import jax.numpy as jnp
from jax import lax
from jax.sharding import PartitionSpec as P

HEAD_DIM = 64
LEVELS = 3
WIN_ROWS = 6
WIN_COLS = 12


def shifted_2(value, axis, steps):
    count = lax.axis_size(axis)
    pairs = [(source, (source + steps) % count) for source in range(count)]
    return lax.ppermute(value, axis, pairs)


def from_partner(value, axis, bit):
    mask = 2**bit
    pairs = [(source, source ^ mask) for source in range(lax.axis_size(axis))]
    return lax.ppermute(value, axis, pairs)


def layer_norm(values, gain):
    wide = values.astype(jnp.float32)
    center = jnp.mean(wide, axis=-1, keepdims=True)
    spread = jnp.mean(jnp.square(wide - center), axis=-1, keepdims=True)
    return ((wide - center) * lax.rsqrt(spread + 1e-05) * gain).astype(jnp.bfloat16)


def to_windows(field):
    levels, rows, cols, width = field.shape
    count = cols // WIN_COLS
    shaped = field.reshape(levels, rows, count, WIN_COLS, width).transpose(2, 0, 1, 3, 4)
    return shaped.reshape(count, levels * rows * WIN_COLS, width)


def from_windows(blocks, levels, rows):
    count, tokens, width = blocks.shape
    shaped = blocks.reshape(count, levels, rows, WIN_COLS, width).transpose(1, 2, 0, 3, 4)
    return shaped.reshape(levels, rows, count * WIN_COLS, width)


def token_labels(row_labels):
    rows = row_labels.shape[0]
    return jnp.broadcast_to(row_labels[None, :, None], (LEVELS, rows, WIN_COLS)).reshape(-1)


def attend(queries_in, keys_in, qkv_weight, proj_weight, allowed):
    count, query_tokens, width = queries_in.shape
    key_tokens = keys_in.shape[1]
    heads = width // HEAD_DIM
    query = jnp.dot(
        queries_in.reshape(-1, width), qkv_weight[:, :width], preferred_element_type=jnp.float32
    )
    query = query.astype(jnp.bfloat16).reshape(count, query_tokens, heads, HEAD_DIM)
    paired = jnp.dot(
        keys_in.reshape(-1, width), qkv_weight[:, width:], preferred_element_type=jnp.float32
    )
    paired = paired.astype(jnp.bfloat16).reshape(count, key_tokens, 2, heads, HEAD_DIM)
    scores = jnp.einsum(
        "wqhd,wkhd->whqk", query, paired[:, :, 0], preferred_element_type=jnp.float32
    )
    scores = scores * HEAD_DIM ** (-0.5)
    scores = jnp.where(allowed[None, None], scores, -1e30)
    highest = jnp.max(scores, axis=-1, keepdims=True)
    expo = jnp.exp(scores - highest)
    weights = (expo / jnp.sum(expo, axis=-1, keepdims=True)).astype(jnp.bfloat16)
    mixed = jnp.einsum(
        "whqk,wkhd->wqhd", weights, paired[:, :, 1], preferred_element_type=jnp.float32
    )
    mixed = mixed.astype(jnp.bfloat16).reshape(count * query_tokens, width)
    return jnp.dot(mixed, proj_weight, preferred_element_type=jnp.float32).reshape(
        count, query_tokens, width
    )


def move_rows(piece, offset):
    return shifted_2(piece, "lat", offset)


def move_cols(piece, offset):
    return shifted_2(piece, "lon", offset)


def move_coarse(piece, offset):
    return shifted_2(piece, "lon", offset)


def move_coarse_rows(piece, offset):
    return shifted_2(piece, "lat", offset)


def roll_ahead(field):
    half_rows = WIN_ROWS // 2
    half_cols = WIN_COLS // 2
    shifted = jnp.concatenate(
        [field[:, :, half_cols:], move_cols(field[:, :, :half_cols], -1)], axis=2
    )
    return jnp.concatenate([shifted[:, half_rows:], move_rows(shifted[:, :half_rows], -1)], axis=1)


def roll_behind(field):
    half_rows = WIN_ROWS // 2
    half_cols = WIN_COLS // 2
    shifted = jnp.concatenate([move_rows(field[:, -half_rows:], 1), field[:, :-half_rows]], axis=1)
    return jnp.concatenate(
        [move_cols(shifted[:, :, -half_cols:], 1), shifted[:, :, :-half_cols]], axis=2
    )


def row_slice(labels, start, length):
    doubled = jnp.concatenate([labels, labels])
    begin = jnp.mod(start, labels.shape[0])
    return lax.dynamic_slice(doubled, (begin,), (length,))


def fine_rolled(field, gain, qkv_weight, proj_weight, labels):
    place = lax.axis_index("lat")
    rolled = roll_ahead(field)
    tokens = token_labels(row_slice(labels, place * WIN_ROWS + WIN_ROWS // 2, WIN_ROWS))
    allowed = tokens[:, None] == tokens[None, :]
    normed = to_windows(layer_norm(rolled, gain))
    branch = from_windows(
        attend(normed, normed, qkv_weight, proj_weight, allowed), LEVELS, WIN_ROWS
    )
    return roll_behind((rolled.astype(jnp.float32) + branch).astype(jnp.bfloat16))


def fine_block(field, gain, qkv_weight, proj_weight, labels):
    return fine_rolled(field, gain, qkv_weight, proj_weight, labels)


def merge_tokens(field, gain, weight):
    stacked = jnp.concatenate(
        [field[:, 0::2, 0::2], field[:, 1::2, 0::2], field[:, 0::2, 1::2], field[:, 1::2, 1::2]],
        axis=-1,
    )
    levels, rows, cols, wide = stacked.shape
    normed = layer_norm(stacked, gain).reshape(-1, wide)
    merged = jnp.dot(normed, weight, preferred_element_type=jnp.float32).astype(jnp.bfloat16)
    return merged.reshape(levels, rows, cols, weight.shape[1])


def coarse_block(merged, gain, qkv_weight, proj_weight):
    parity = lax.axis_index("lat") % 2
    half_rows = WIN_ROWS // 2
    half_cols = WIN_COLS // 2
    shifted = jnp.concatenate(
        [merged[:, :, half_cols:], move_coarse(merged[:, :, :half_cols], -1)], axis=2
    )
    ahead = move_coarse_rows(shifted, -1)
    partner = from_partner(ahead, "lat", 0)
    is_lower = parity == 0
    lower = jnp.where(is_lower, ahead, partner)
    upper = jnp.where(is_lower, partner, ahead)
    window = jnp.concatenate([lower, upper], axis=1)
    normed = layer_norm(window, gain)
    queries = lax.dynamic_slice_in_dim(normed, parity * half_rows, half_rows, 1)
    query_count = LEVELS * half_rows * WIN_COLS
    allowed = jnp.ones((query_count, 2 * query_count), jnp.bool_)
    attended = attend(to_windows(queries), to_windows(normed), qkv_weight, proj_weight, allowed)
    branch = from_windows(attended, LEVELS, half_rows)
    owned = (ahead.astype(jnp.float32) + branch).astype(jnp.bfloat16)
    back = move_coarse_rows(owned, 1)
    return jnp.concatenate(
        [move_coarse(back[:, :, -half_cols:], 1), back[:, :, :-half_cols]], axis=2
    )


def split_tokens(coarse, gain, weight, skipped):
    levels, rows, cols, wide = coarse.shape
    normed = layer_norm(coarse, gain).reshape(-1, wide)
    spread = jnp.dot(normed, weight, preferred_element_type=jnp.float32)
    width = weight.shape[1] // 4
    placed = spread.reshape(levels, rows, cols, 2, 2, width).transpose(0, 1, 4, 2, 3, 5)
    placed = placed.reshape(levels, 2 * rows, 2 * cols, width)
    return (skipped.astype(jnp.float32) + placed).astype(jnp.bfloat16)


def body(
    latent,
    band_labels,
    gain_first,
    qkv_first,
    proj_first,
    merge_gain,
    merge_weight,
    gain_coarse,
    qkv_coarse,
    proj_coarse,
    split_gain,
    split_weight,
    gain_last,
    qkv_last,
    proj_last,
):
    first = fine_block(latent, gain_first, qkv_first, proj_first, band_labels)
    merged = merge_tokens(first, merge_gain, merge_weight)
    coarse = coarse_block(merged, gain_coarse, qkv_coarse, proj_coarse)
    joined = split_tokens(coarse, split_gain, split_weight, first)
    return fine_block(joined, gain_last, qkv_last, proj_last, band_labels)


def solution(mesh):
    return jax.shard_map(
        body,
        mesh=mesh,
        in_specs=(
            P("rep", "lat", "lon", None),
            P(),
            P(),
            P(),
            P(),
            P(),
            P(),
            P(),
            P(),
            P(),
            P(),
            P(),
            P(),
            P(),
            P(),
        ),
        out_specs=P("rep", "lat", "lon", None),
        check_vma=False,
    )
```

profile of v0, /device:TPU:0, one launch (start us, length us, event | category | flops | bytes accessed | tf_op | source)
XLA Modules:
  0.0 550.1 jit_solution(4987930602541317460)
XLA Ops:
  12.6 18.6 %collective-permute-done.1 = bf16[3,3,96,512]{3,2,1,0:T(8,128)(2,1)} collective-permute-done((bf16[3,3,96,512]{3,2,1,0:T(8,128)(2,1)}, bf16[3,3,96,512]{3,2,1,0:T(8,128)(2,1)}, u32[]{:S(2)}, u32[]{:S(2)}) %collective-permute-start.1) | collective-permute-done | bytes 884768 | tf_op jit(solution)/shard_map/ppermute | solution.py:15
  44.7 5.7 %convolution_convert_fusion.1 = bf16[1728,1024]{1,0:T(8,128)(2,1)} fusion(bf16[1728,512]{1,0:T(8,128)(2,1)} %reshape_reshape.8, bf16[512,1536]{1,0:T(8,128)(2,1)} %param.18), kind=kOutput, calls=%fused_computation.39 | convolution fusion | flops 1813708800 | bytes 6356992 | tf_op jit(solution)/shard_map/dot_general | solution.py:57
  53.8 9.9 %reshape.283 = bf16[8,216,2,8,64]{4,3,2,1,0:T(8,128)(2,1)} reshape(bf16[1728,1024]{1,0:T(8,128)(2,1)} %convolution_convert_fusion.1) | data formatting | bytes 7077888 | tf_op jit(solution)/shard_map/reshape | solution.py:60
  63.7 6.5 %fusion.135 = (bf16[8,216,1,8,64]{4,3,2,1,0:T(8,128)(2,1)}, bf16[8,216,1,8,64]{4,3,2,1,0:T(8,128)(2,1)}) fusion(bf16[8,216,2,8,64]{4,3,2,1,0:T(8,128)(2,1)} %reshape.283), kind=kLoop, calls=%fused_computation.167 | loop fusion | bytes 7077888 | tf_op jit(solution)/shard_map/slice | solution.py:70
  75.0 5.8 %reshape.277 = bf16[8,216,8,64]{3,2,1,0:T(8,128)(2,1)} reshape(bf16[1728,512]{1,0:T(8,128)(2,1)} %convolution_convert_fusion.3) | data formatting | bytes 3538944 | tf_op jit(solution)/shard_map/reshape | solution.py:56
  80.8 9.8 %fusion.28 = f32[8,8,216,216]{2,3,1,0:T(8,128)} fusion(bf16[8,216,8,64]{3,2,1,0:T(8,128)(2,1)} %reshape.277, bf16[8,216,1,8,64]{1,4,3,0,2:T(8,128)(2,1)} %copy.90), kind=kOutput, calls=%fused_computation.50 | convolution fusion | flops 382205952 | bytes 15482880 | tf_op jit(solution)/shard_map/wqhd,wkhd->whqk/dot_general | solution.py:61
  90.6 7.9 %fusion.138 = f32[8,8,216]{2,1,0:T(8,128)S(1)} fusion(pred[216,216]{0,1:T(8,128)(4,1)S(1)} %broadcast_compare_fusion, bf16[8,216,1,8,64]{1,4,3,0,2:T(8,128)(2,1)} %copy.90, bf16[8,216,8,64]{3,2,1,0:T(8,128)(2,1)} %reshape.277), kind=kOutput, calls=%fused_computation.170 | convolution fusion | flops 394150112 | bytes 3640896 | tf_op jit(solution)/shard_map/sub | solution.py:67
  98.5 5.2 copy.89
  103.7 11.3 %convert_bitcast_fusion.1 = bf16[8,216,8,64]{1,3,2,0:T(8,128)(2,1)} fusion(f32[8,8,216]{2,1,0:T(8,128)S(1)} %fusion.138, bf16[8,216,1,8,64]{1,4,3,0,2:T(8,128)(2,1)} %copy.89, f32[8,8,216,216]{2,3,1,0:T(8,128)} %fusion.28, pred[216,216]{0,1:T(8,128)(4,1)S(1)} %broadcast_compare_fusion), kind=kOutput, calls=%fused_computation.81 | convolution fusion | flops 398034656 | bytes 15584832 | tf_op jit(solution)/shard_map/whqk,wkhd->wqhd/dot_general | solution.py:69
  119.8 6.1 %reshape.278 = bf16[8,3,6,12,512]{4,3,2,1,0:T(8,128)(2,1)} reshape(bf16[8,216,8,64]{3,2,1,0:T(8,128)(2,1)} %copy.72) | data formatting | bytes 3538944 | tf_op jit(solution)/shard_map/dot_general | solution.py:73
  140.4 23.6 %collective-permute-done.2 = bf16[3,3,96,512]{3,2,1,0:T(8,128)(2,1)S(1)} collective-permute-done((bf16[3,3,96,512]{3,2,1,0:T(8,128)(2,1)S(1)}, bf16[3,3,96,512]{3,2,1,0:T(8,128)(2,1)S(1)}, u32[]{:S(2)}, u32[]{:S(2)}) %collective-permute-start.2) | collective-permute-done | bytes 884768 | tf_op jit(solution)/shard_map/ppermute | solution.py:15
  185.5 5.8 %slice.123 = bf16[3,3,48,512]{3,2,1,0:T(8,128)(2,1)} slice(bf16[3,6,96,512]{3,2,1,0:T(8,128)(2,1)} %fusion.63), slice={[0:3:1], [1:6:2], [1:96:2], [0:512:1]} | slice | bytes 884736 | tf_op jit(solution)/shard_map/slice | solution.py:136
  203.5 20.6 %collective-permute-done.5 = bf16[3,3,48,1024]{3,2,1,0:T(8,128)(2,1)S(1)} collective-permute-done((bf16[3,3,48,1024]{3,2,1,0:T(8,128)(2,1)S(1)}, bf16[3,3,48,1024]{3,2,1,0:T(8,128)(2,1)S(1)}, u32[]{:S(2)}, u32[]{:S(2)}) %collective-permute-start.5) | collective-permute-done | bytes 884768 | tf_op jit(solution)/shard_map/ppermute | solution.py:15
  225.1 20.7 %collective-permute-done.6 = bf16[3,3,48,1024]{3,2,1,0:T(8,128)(2,1)} collective-permute-done((bf16[3,3,48,1024]{3,2,1,0:T(8,128)(2,1)S(1)}, bf16[3,3,48,1024]{3,2,1,0:T(8,128)(2,1)}, u32[]{:S(2)}, u32[]{:S(2)}) %collective-permute-start.6) | collective-permute-done | bytes 884768 | tf_op jit(solution)/shard_map/ppermute | solution.py:21
  276.7 8.4 %fusion.32 = bf16[864,2048]{1,0:T(8,128)(2,1)} fusion(bf16[864,1024]{1,0:T(8,128)(2,1)} %reshape_reshape.18, bf16[1024,3072]{1,0:T(8,128)(2,1)} %param.23), kind=kOutput, calls=%fused_computation.57 | convolution fusion | flops 3625648128 | bytes 9502720 | tf_op jit(solution)/shard_map/dot_general | solution.py:57
  285.0 11.1 %reshape.284 = bf16[4,216,2,16,64]{4,3,2,1,0:T(8,128)(2,1)} reshape(bf16[864,2048]{1,0:T(8,128)(2,1)} %fusion.32) | data formatting | bytes 7077888 | tf_op jit(solution)/shard_map/reshape | solution.py:60
  296.1 7.2 %fusion.134 = (bf16[4,216,1,16,64]{4,3,2,1,0:T(8,128)(2,1)}, bf16[4,216,1,16,64]{4,3,2,1,0:T(8,128)(2,1)}) fusion(bf16[4,216,2,16,64]{4,3,2,1,0:T(8,128)(2,1)} %reshape.284), kind=kLoop, calls=%fused_computation.166 | loop fusion | bytes 7077888 | tf_op jit(solution)/shard_map/slice | solution.py:70
  303.3 5.6 %copy.92 = bf16[4,216,1,16,64]{1,4,3,0,2:T(8,128)(2,1)} copy(bf16[4,216,1,16,64]{4,3,2,1,0:T(8,128)(2,1)} %get-tuple-element.8) | data formatting | bytes 3538944
  318.0 5.4 copy.91
  339.2 22.2 %collective-permute-done.7 = bf16[3,3,48,1024]{3,2,1,0:T(8,128)(2,1)S(1)} collective-permute-done((bf16[3,3,48,1024]{3,2,1,0:T(8,128)(2,1)S(1)}, bf16[3,3,48,1024]{3,2,1,0:T(8,128)(2,1)S(1)}, u32[]{:S(2)}, u32[]{:S(2)}) %collective-permute-start.7) | collective-permute-done | bytes 884768 | tf_op jit(solution)/shard_map/ppermute | solution.py:15
  361.5 6.7 %copy.76 = bf16[2048,1024]{1,0:T(8,128)(2,1)} copy(bf16[2048,1024]{0,1:T(8,128)(2,1)} %bitcast.125) | data formatting | bytes 8388608 | tf_op jit(solution)/shard_map/dot_general | solution.py:174
  378.1 5.5 %reshape.268 = f32[3,6,96,512]{3,2,1,0:T(8,128)} reshape(f32[3,3,2,48,2,512]{5,4,3,2,1,0:T(2,128)} %copy.52) | data formatting | bytes 7077888 | tf_op jit(solution)/shard_map/reshape | solution.py:177
  393.8 20.4 %collective-permute-done.10 = bf16[3,3,96,512]{3,2,1,0:T(8,128)(2,1)S(1)} collective-permute-done((bf16[3,3,96,512]{3,2,1,0:T(8,128)(2,1)}, bf16[3,3,96,512]{3,2,1,0:T(8,128)(2,1)S(1)}, u32[]{:S(2)}, u32[]{:S(2)}) %collective-permute-start.10) | collective-permute-done | bytes 884768 | tf_op jit(solution)/shard_map/ppermute | solution.py:15
  424.8 5.7 %convolution_convert_fusion = bf16[1728,1024]{1,0:T(8,128)(2,1)} fusion(bf16[1728,512]{1,0:T(8,128)(2,1)} %reshape_reshape.20, bf16[512,1536]{1,0:T(8,128)(2,1)} %param.28), kind=kOutput, calls=%fused_computation.38 | convolution fusion | flops 1813708800 | bytes 6356992 | tf_op jit(solution)/shard_map/dot_general | solution.py:57
  433.8 9.9 %reshape.285 = bf16[8,216,2,8,64]{4,3,2,1,0:T(8,128)(2,1)} reshape(bf16[1728,1024]{1,0:T(8,128)(2,1)} %convolution_convert_fusion) | data formatting | bytes 7077888 | tf_op jit(solution)/shard_map/reshape | solution.py:60
  443.7 6.5 %fusion.133 = (bf16[8,216,1,8,64]{4,3,2,1,0:T(8,128)(2,1)}, bf16[8,216,1,8,64]{4,3,2,1,0:T(8,128)(2,1)}) fusion(bf16[8,216,2,8,64]{4,3,2,1,0:T(8,128)(2,1)} %reshape.285), kind=kLoop, calls=%fused_computation.165 | loop fusion | bytes 7077888 | tf_op jit(solution)/shard_map/slice | solution.py:70
  455.1 5.7 %reshape.281 = bf16[8,216,8,64]{3,2,1,0:T(8,128)(2,1)} reshape(bf16[1728,512]{1,0:T(8,128)(2,1)} %convolution_convert_fusion.2) | data formatting | bytes 3538944 | tf_op jit(solution)/shard_map/reshape | solution.py:56
  460.8 9.8 %fusion.26 = f32[8,8,216,216]{2,3,1,0:T(8,128)} fusion(bf16[8,216,8,64]{3,2,1,0:T(8,128)(2,1)} %reshape.281, bf16[8,216,1,8,64]{1,4,3,0,2:T(8,128)(2,1)} %copy.94), kind=kOutput, calls=%fused_computation.48 | convolution fusion | flops 382205952 | bytes 15482880 | tf_op jit(solution)/shard_map/wqhd,wkhd->whqk/dot_general | solution.py:61
  470.6 7.9 %fusion.144 = f32[8,8,216]{2,1,0:T(8,128)S(1)} fusion(pred[216,216]{0,1:T(8,128)(4,1)S(1)} %copy-done.12, bf16[8,216,1,8,64]{1,4,3,0,2:T(8,128)(2,1)} %copy.94, bf16[8,216,8,64]{3,2,1,0:T(8,128)(2,1)} %reshape.281), kind=kOutput, calls=%fused_computation.172 | convolution fusion | flops 394150112 | bytes 3640896 | tf_op jit(solution)/shard_map/sub | solution.py:67
  483.5 11.4 %convert_bitcast_fusion = bf16[8,216,8,64]{1,3,2,0:T(8,128)(2,1)} fusion(f32[8,8,216]{2,1,0:T(8,128)S(1)} %fusion.144, bf16[8,216,1,8,64]{1,4,3,0,2:T(8,128)(2,1)} %copy.93, f32[8,8,216,216]{2,3,1,0:T(8,128)} %fusion.26, pred[216,216]{0,1:T(8,128)(4,1)S(1)} %copy-done.12), kind=kOutput, calls=%fused_computation.78 | convolution fusion | flops 398034656 | bytes 15584832 | tf_op jit(solution)/shard_map/whqk,wkhd->wqhd/dot_general | solution.py:69
  499.7 6.1 %reshape.282 = bf16[8,3,6,12,512]{4,3,2,1,0:T(8,128)(2,1)} reshape(bf16[8,216,8,64]{3,2,1,0:T(8,128)(2,1)} %copy.79) | data formatting | bytes 3538944 | tf_op jit(solution)/shard_map/dot_general | solution.py:73
  519.6 23.6 %collective-permute-done.11 = bf16[3,3,96,512]{3,2,1,0:T(8,128)(2,1)S(1)} collective-permute-done((bf16[3,3,96,512]{3,2,1,0:T(8,128)(2,1)S(1)}, bf16[3,3,96,512]{3,2,1,0:T(8,128)(2,1)S(1)}, u32[]{:S(2)}, u32[]{:S(2)}) %collective-permute-start.11) | collective-permute-done | bytes 884768 | tf_op jit(solution)/shard_map/ppermute | solution.py:15
  (160 shorter events, 212.8 us)
Async XLA Ops:
  0.0 333.8 %copy-start = (bf16[1024,1024]{1,0:T(8,128)(2,1)S(1)}, bf16[1024,1024]{1,0:T(8,128)(2,1)}, u32[]{:S(2)}) copy-start(bf16[1024,1024]{1,0:T(8,128)(2,1)} %param.24) | copy-start | bytes 6291460
  1.1 9.8 %copy-start.18 = (s32[24]{0:T(128)S(1)}, s32[24]{0:T(128)}, u32[]{:S(2)}) copy-start(s32[24]{0:T(128)} %param.16) | copy-start | bytes 292
  1.1 5.1 collective-permute-start
  7.3 23.8 %collective-permute-start.1 = (bf16[3,3,96,512]{3,2,1,0:T(8,128)(2,1)}, bf16[3,3,96,512]{3,2,1,0:T(8,128)(2,1)}, u32[]{:S(2)}, u32[]{:S(2)}) collective-permute-start(bf16[3,3,96,512]{3,2,1,0:T(8,128)(2,1)} %get-tuple-element.14), channel_id=1, source_target_pairs={{0,24},{8,0},{16,8},{24,16},{1,25},{9,1},{17,9},{25,17},{2,26},{10... | collective-permute-start | bytes 2654216 | tf_op jit(solution)/shard_map/ppermute | solution.py:15
  11.3 92.4 %copy-start.11 = (pred[216,216]{0,1:T(8,128)(4,1)}, pred[216,216]{0,1:T(8,128)(4,1)S(1)}, u32[]{:S(2)}) copy-start(pred[216,216]{0,1:T(8,128)(4,1)S(1)} %broadcast_compare_fusion) | copy-start | bytes 139972
  11.4 25.6 %copy-start.14 = (f32[512]{0:T(512)S(1)}, f32[512]{0:T(512)}, u32[]{:S(2)}) copy-start(f32[512]{0:T(512)} %param.17) | copy-start | bytes 6148
  44.7 5.7 %copy-start.7 = (bf16[1728,512]{1,0:T(8,128)(2,1)S(1)}, bf16[1728,512]{1,0:T(8,128)(2,1)}, u32[]{:S(2)}) copy-start(bf16[1728,512]{1,0:T(8,128)(2,1)} %reshape_reshape.8) | copy-start | bytes 5308420
  119.8 6.1 %copy-start.9 = (bf16[512,512]{1,0:T(8,128)(2,1)S(1)}, bf16[512,512]{1,0:T(8,128)(2,1)}, u32[]{:S(2)}) copy-start(bf16[512,512]{1,0:T(8,128)(2,1)} %param.19) | copy-start | bytes 1572868
  139.9 24.1 %collective-permute-start.2 = (bf16[3,3,96,512]{3,2,1,0:T(8,128)(2,1)S(1)}, bf16[3,3,96,512]{3,2,1,0:T(8,128)(2,1)S(1)}, u32[]{:S(2)}, u32[]{:S(2)}) collective-permute-start(bf16[3,3,96,512]{3,2,1,0:T(8,128)(2,1)S(1)} %get-tuple-element.21), channel_id=1, source_target_pairs={{0,8},{8,16},{16,24},{24,0},{1,9},{9,17},{17,25},{25,1},{2,10},{10... | collective-permute-start | bytes 2654216 | tf_op jit(solution)/shard_map/ppermute | solution.py:15
  164.0 4.6 collective-permute-start.3
  170.7 23.7 %copy-start.16 = (f32[2048]{0:T(1024)S(1)}, f32[2048]{0:T(1024)}, u32[]{:S(2)}) copy-start(f32[2048]{0:T(1024)} %param.20) | copy-start | bytes 24580
  198.8 2.7 collective-permute-start.4
  201.7 22.4 %collective-permute-start.5 = (bf16[3,3,48,1024]{3,2,1,0:T(8,128)(2,1)S(1)}, bf16[3,3,48,1024]{3,2,1,0:T(8,128)(2,1)S(1)}, u32[]{:S(2)}, u32[]{:S(2)}) collective-permute-start(bf16[3,3,48,1024]{3,2,1,0:T(8,128)(2,1)S(1)} %pad_maximum_fusion.8), channel_id=1, source_target_pairs={{0,24},{8,0},{16,8},{24,16},{1,25},{9,1},{17,9},{25,17},{2,26},{10... | collective-permute-start | bytes 2654216 | tf_op jit(solution)/shard_map/ppermute | solution.py:15
  224.1 0.9 copy-start.5
  224.1 21.6 %collective-permute-start.6 = (bf16[3,3,48,1024]{3,2,1,0:T(8,128)(2,1)S(1)}, bf16[3,3,48,1024]{3,2,1,0:T(8,128)(2,1)}, u32[]{:S(2)}, u32[]{:S(2)}) collective-permute-start(bf16[3,3,48,1024]{3,2,1,0:T(8,128)(2,1)S(1)} %collective-permute-done.5), channel_id=1, source_target_pairs={{0,8},{8,0},{16,24},{24,16},{1,9},{9,1},{17,25},{25,17},{2,10},{10... | collective-permute-start | bytes 2654216 | tf_op jit(solution)/shard_map/ppermute | solution.py:21
  247.3 0.9 copy-start.3
  248.2 6.1 %copy-start.13 = (f32[1024]{0:T(1024)S(1)}, f32[1024]{0:T(1024)}, u32[]{:S(2)}) copy-start(f32[1024]{0:T(1024)} %param.22) | copy-start | bytes 12292
  261.5 7.5 %copy-start.4 = (bf16[3,3,4,12,1024]{4,3,2,1,0:T(8,128)(2,1)S(1)}, bf16[3,3,4,12,1024]{4,3,2,1,0:T(8,128)(2,1)}, u32[]{:S(2)}) copy-start(bf16[3,3,4,12,1024]{4,3,2,1,0:T(8,128)(2,1)} %concatenate.91) | copy-start | bytes 2654212
  335.2 3.3 copy-start.6
  338.9 22.5 %collective-permute-start.7 = (bf16[3,3,48,1024]{3,2,1,0:T(8,128)(2,1)S(1)}, bf16[3,3,48,1024]{3,2,1,0:T(8,128)(2,1)S(1)}, u32[]{:S(2)}, u32[]{:S(2)}) collective-permute-start(bf16[3,3,48,1024]{3,2,1,0:T(8,128)(2,1)S(1)} %add_convert_fusion.1), channel_id=1, source_target_pairs={{0,8},{8,16},{16,24},{24,0},{1,9},{9,17},{17,25},{25,1},{2,10},{10... | collective-permute-start | bytes 2654216 | tf_op jit(solution)/shard_map/ppermute | solution.py:15
  361.4 6.7 %collective-permute-start.8 = (bf16[3,3,6,1024]{3,2,1,0:T(8,128)(2,1)S(1)}, bf16[3,3,6,1024]{3,2,1,0:T(8,128)(2,1)S(1)}, u32[]{:S(2)}, u32[]{:S(2)}) collective-permute-start(bf16[3,3,6,1024]{3,2,1,0:T(8,128)(2,1)S(1)} %slice.154), channel_id=1, source_target_pairs={{0,2},{2,4},{4,6},{6,0},{1,3},{3,5},{5,7},{7,1},{8,10},{10,12},{12... | collective-permute-start | bytes 331784 | tf_op jit(solution)/shard_map/ppermute | solution.py:15
  361.5 7.6 %copy-start.17 = (f32[1024]{0:T(1024)S(1)}, f32[1024]{0:T(1024)}, u32[]{:S(2)}) copy-start(f32[1024]{0:T(1024)} %param.25) | copy-start | bytes 12292
  378.1 5.6 %copy-start.2 = (bf16[3,6,96,512]{3,2,1,0:T(8,128)(2,1)S(1)}, bf16[3,6,96,512]{3,2,1,0:T(8,128)(2,1)}, u32[]{:S(2)}) copy-start(bf16[3,6,96,512]{3,2,1,0:T(8,128)(2,1)} %fusion.63) | copy-start | bytes 5308420
  386.3 4.4 collective-permute-start.9
  391.9 22.3 %collective-permute-start.10 = (bf16[3,3,96,512]{3,2,1,0:T(8,128)(2,1)}, bf16[3,3,96,512]{3,2,1,0:T(8,128)(2,1)S(1)}, u32[]{:S(2)}, u32[]{:S(2)}) collective-permute-start(bf16[3,3,96,512]{3,2,1,0:T(8,128)(2,1)} %get-tuple-element.12), channel_id=1, source_target_pairs={{0,24},{8,0},{16,8},{24,16},{1,25},{9,1},{17,9},{25,17},{2,26},{10... | collective-permute-start | bytes 2654216 | tf_op jit(solution)/shard_map/ppermute | solution.py:15
  393.6 23.2 %copy-start.15 = (f32[512]{0:T(512)S(1)}, f32[512]{0:T(512)}, u32[]{:S(2)}) copy-start(f32[512]{0:T(512)} %param.27) | copy-start | bytes 6148
  424.8 5.7 %copy-start.8 = (bf16[1728,512]{1,0:T(8,128)(2,1)S(1)}, bf16[1728,512]{1,0:T(8,128)(2,1)}, u32[]{:S(2)}) copy-start(bf16[1728,512]{1,0:T(8,128)(2,1)} %reshape_reshape.20) | copy-start | bytes 5308420
  460.8 9.8 %copy-start.12 = (pred[216,216]{0,1:T(8,128)(4,1)S(1)}, pred[216,216]{0,1:T(8,128)(4,1)}, u32[]{:S(2)}) copy-start(pred[216,216]{0,1:T(8,128)(4,1)} %copy-done.11) | copy-start | bytes 139972
  499.7 6.1 %copy-start.10 = (bf16[512,512]{1,0:T(8,128)(2,1)S(1)}, bf16[512,512]{1,0:T(8,128)(2,1)}, u32[]{:S(2)}) copy-start(bf16[512,512]{1,0:T(8,128)(2,1)} %param.29) | copy-start | bytes 1572868
  519.3 30.6 %copy-start.1 = (bf16[1024,1024]{1,0:T(8,128)(2,1)S(1)}, bf16[1024,1024]{1,0:T(8,128)(2,1)}, u32[]{:S(2)}) copy-start(bf16[1024,1024]{1,0:T(8,128)(2,1)} %param.24) | copy-start | bytes 6291460
  519.5 23.7 %collective-permute-start.11 = (bf16[3,3,96,512]{3,2,1,0:T(8,128)(2,1)S(1)}, bf16[3,3,96,512]{3,2,1,0:T(8,128)(2,1)S(1)}, u32[]{:S(2)}, u32[]{:S(2)}) collective-permute-start(bf16[3,3,96,512]{3,2,1,0:T(8,128)(2,1)S(1)} %get-tuple-element.17), channel_id=1, source_target_pairs={{0,8},{8,16},{16,24},{24,0},{1,9},{9,17},{17,25},{25,1},{2,10},{10... | collective-permute-start | bytes 2654216 | tf_op jit(solution)/shard_map/ppermute | solution.py:15
  543.2 4.6 collective-permute-start.12
where the time goes:
time: 560 us; the launch traced here: 550 us
  local copies, waits for them, and re-layouts  217 us (39%)
  waiting for transfers between devices  163 us (29%)
  matrix products  114 us (20%)
  other arithmetic  42.1 us (8%)
  starting transfers between devices  12.4 us (2%)
    ppermute x12, waiting for transfers between devices, shifted_2(): return lax.ppermute(value, axis, pairs)  143 us
    unnamed x44, local copies, waits for them, and re-layouts  32.5 us
    reshape x3, local copies, waits for them, and re-layouts, attend(): paired.astype(jnp.bfloat16).reshape(count, key_tokens, 2, heads, HEAD_DIM)  30.9 us
    dot_general x3, matrix products, attend(): jnp.einsum('whqk,wkhd->wqhd', weights, paired[:, :, 1], preferred_element...  27.8 us
    dot_general x6, local copies, waits for them, and re-layouts, attend(): jnp.dot(mixed, proj_weight, preferred_element_type=jnp.float32)  27.1 us
    dot_general x3, matrix products, attend(): jnp.einsum('wqhd,wkhd->whqk', query, paired[:, :, 0], preferred_element_t...  23.8 us
    ppermute x1, waiting for transfers between devices, from_partner(): return lax.ppermute(value, axis, pairs)  20.7 us
    slice x3, local copies, waits for them, and re-layouts, attend(): paired[:, :, 1]  20.2 us
  transfers between devices with their start and end apart: 13, of which 12 were waited for; matrix products, arithmetic and copies ran while one was open for 2% of the time, Pallas kernels for 0%

commit v1 on v0

v1 whole, which is shorter than its diff:
```python
import functools
import math
import jax
import jax.numpy as jnp
from jax import lax
from jax.experimental import pallas as pl
from jax.experimental.pallas import tpu as pltpu
from jax.sharding import PartitionSpec as P

HEAD_DIM = 64
LEVELS = 3
WIN_ROWS = 6
WIN_COLS = 12
HALF_ROWS = WIN_ROWS // 2
HALF_COLS = WIN_COLS // 2
TOKENS = LEVELS * WIN_ROWS * WIN_COLS
LANES = 128
SCALE = HEAD_DIM**-0.5 * math.log2(math.e)
PARAMS = pltpu.CompilerParams(vmem_limit_bytes=60 * 1024 * 1024)


def norm(wide, gain):
    center = jnp.mean(wide, axis=-1, keepdims=True)
    moved = wide - center
    spread = jnp.mean(jnp.square(moved), axis=-1, keepdims=True)
    return (moved * lax.rsqrt(spread + 1e-05) * gain).astype(jnp.bfloat16)


def rounded(value):
    return value.astype(jnp.bfloat16).astype(jnp.float32)


def attend(x, gain, qkv_ref, proj_ref, bias, qkv_s, mix_s):
    width = x.shape[1]
    normed = norm(x, gain)
    for third in range(3):
        part = jnp.dot(
            normed,
            qkv_ref[:, third * width : (third + 1) * width],
            preferred_element_type=jnp.float32,
        )
        qkv_s[:, third * width : (third + 1) * width] = part.astype(jnp.bfloat16)
    pair = 2 * HEAD_DIM
    low = lax.broadcasted_iota(jnp.int32, (TOKENS, pair), 1) < HEAD_DIM
    ones = jnp.ones((TOKENS, pair), jnp.bfloat16)
    zeros = jnp.zeros((TOKENS, pair), jnp.bfloat16)
    for j in range(width // pair):
        q = qkv_s[:, j * pair : (j + 1) * pair]
        k = qkv_s[:, width + j * pair : width + (j + 1) * pair]
        v = qkv_s[:, 2 * width + j * pair : 2 * width + (j + 1) * pair]
        summed = jnp.concatenate([v, ones], axis=1)
        parts = []
        for keep in (low, ~low):
            s = lax.dot_general(
                q,
                jnp.where(keep, k, zeros),
                (((1,), (1,)), ((), ())),
                preferred_element_type=jnp.float32,
            )
            s = s * SCALE
            if bias is not None:
                s = s + bias
            p = jnp.exp2(s - jnp.max(s, axis=-1, keepdims=True)).astype(jnp.bfloat16)
            r = jnp.dot(p, summed, preferred_element_type=jnp.float32)
            parts.append(r[:, :pair] / r[:, pair:])
        mix_s[:, j * pair : (j + 1) * pair] = jnp.where(low, parts[0], parts[1]).astype(
            jnp.bfloat16
        )
    return rounded(x + jnp.dot(mix_s[...], proj_ref[...], preferred_element_type=jnp.float32))


def row_of(dim):
    t = lax.broadcasted_iota(jnp.int32, (TOKENS, TOKENS), dim)
    group = (t * 43691) >> 19
    return group - WIN_ROWS * ((group * 43691) >> 18)


def make_bias(labels_ref, first_row):
    count = labels_ref.shape[0]
    rows = [row_of(0), row_of(1)]
    marks = [jnp.zeros((TOKENS, TOKENS), jnp.int32) for _ in rows]
    for r in range(WIN_ROWS):
        label = labels_ref[lax.rem(first_row + r + count, count)]
        marks = [jnp.where(row == r, label, mark) for row, mark in zip(rows, marks)]
    return jnp.where(marks[0] == marks[1], 0.0, -1e30)


def strip_of(place, center):
    odd = lax.rem(place, 2) == 1
    is_left = odd if center else jnp.logical_not(odd)
    first_row = WIN_ROWS * place + jnp.where(is_left, HALF_ROWS, -HALF_ROWS)
    return is_left, first_row


def load(win_s, w):
    return jnp.concatenate([win_s[w, c] for c in range(win_s.shape[1])], axis=1)


def store(win_s, w, start, value):
    for c in range(win_s.shape[1]):
        win_s[w, c, start : start + value.shape[0], :] = value[:, c * LANES : (c + 1) * LANES]


def put(win_s, group, start, value):
    at, done = start, 0
    while done < value.shape[0]:
        w, c = divmod(at, WIN_COLS)
        size = min(WIN_COLS - c, value.shape[0] - done)
        store(win_s, w, group * WIN_COLS + c, value[done : done + size])
        at, done = at + size, done + size


def merge_rows(upper, lower, gain, weight):
    levels, cols, wide = upper.shape
    a = upper.reshape(levels * cols, wide)
    b = lower.reshape(levels * cols, wide)
    half = wide // 2
    stacked = jnp.concatenate([a[:, :half], b[:, :half], a[:, half:], b[:, half:]], axis=1)
    out = jnp.dot(norm(stacked, gain), weight, preferred_element_type=jnp.float32)
    return out.astype(jnp.bfloat16).astype(jnp.float32).reshape(levels, cols, wide)


def wide(ref, index):
    return ref[index].astype(jnp.float32)


def first_kernel(
    center,
    half,
    place_ref,
    labels_ref,
    x_ref,
    lon_ref,
    main_ref,
    second_ref,
    gain_ref,
    qkv_ref,
    proj_ref,
    mgain_ref,
    mweight_ref,
    out_ref,
    upper_ref,
    lower_ref,
    win_s,
    qkv_s,
    mix_s,
    bias_s,
):
    is_left, first_row = strip_of(place_ref[0], center)
    cut = x_ref.shape[2] - half - HALF_COLS
    span = half + WIN_COLS

    @pl.when(is_left)
    def _():
        for l in range(LEVELS):
            for r in range(HALF_ROWS):
                own = x_ref[l, HALF_ROWS + r].astype(jnp.float32)
                put(win_s, l * WIN_ROWS + r, 0, own[HALF_COLS : HALF_COLS + span])
                group = l * WIN_ROWS + HALF_ROWS + r
                put(win_s, group, 0, main_ref[l, r].astype(jnp.float32))
                put(win_s, group, cut, second_ref[l, r].astype(jnp.float32))

    @pl.when(jnp.logical_not(is_left))
    def _():
        for l in range(LEVELS):
            for r in range(HALF_ROWS):
                group = l * WIN_ROWS + r
                put(win_s, group, 0, main_ref[l, r].astype(jnp.float32))
                put(win_s, group, cut, second_ref[l, r].astype(jnp.float32))
                group = l * WIN_ROWS + HALF_ROWS + r
                own = x_ref[l, r].astype(jnp.float32)
                put(win_s, group, 0, own[HALF_COLS + half :])
                put(win_s, group, cut, lon_ref[l, r].astype(jnp.float32))

    bias_s[...] = make_bias(labels_ref, first_row)

    def window(w, carry):
        done = attend(
            load(win_s, w), gain_ref[...], qkv_ref, proj_ref, bias_s[...], qkv_s, mix_s
        )
        store(win_s, w, 0, done)
        return carry

    lax.fori_loop(0, win_s.shape[0], window, 0)

    groups = win_s.shape[1]
    for l in range(LEVELS):
        for r in range(WIN_ROWS):
            base = (l * WIN_ROWS + r) * WIN_COLS
            for parity in range(2):
                for c in range(groups):
                    pieces = []
                    for w in range(win_s.shape[0]):
                        skip = HALF_COLS if w == 0 else 0
                        size = HALF_COLS // 2 if w in (0, win_s.shape[0] - 1) else HALF_COLS
                        pieces.append(win_s[w, c, pl.ds(base + skip + parity, size, stride=2), :])
                    at = (parity * groups + c) * LANES
                    out_ref[r, l, :, at : at + LANES] = jnp.concatenate(pieces, axis=0).astype(
                        jnp.bfloat16
                    )
    upper_ref[0] = out_ref[0]
    lower_ref[1] = out_ref[WIN_ROWS - 1]
    upper_ref[1] = merge_rows(
        wide(out_ref, 1), wide(out_ref, 2), mgain_ref[...], mweight_ref[...]
    ).astype(jnp.bfloat16)
    lower_ref[0] = merge_rows(
        wide(out_ref, 3), wide(out_ref, 4), mgain_ref[...], mweight_ref[...]
    ).astype(jnp.bfloat16)


def spread_add(spread, upper, lower):
    width = spread.shape[-1] // 4
    parts = [spread[..., i * width : (i + 1) * width] for i in range(4)]
    top = upper + jnp.concatenate([parts[0], parts[2]], axis=-1)
    bottom = lower + jnp.concatenate([parts[1], parts[3]], axis=-1)
    return top.astype(jnp.bfloat16), bottom.astype(jnp.bfloat16)


def coarse_kernel(
    first_ref,
    upper_ref,
    lower_ref,
    prev_ref,
    next_ref,
    mgain_ref,
    mweight_ref,
    gain_ref,
    qkv_ref,
    proj_ref,
    sgain_ref,
    sweight_ref,
    out_ref,
    to_prev_ref,
    to_next_ref,
    edge_ref,
    win_s,
    spread_s,
    qkv_s,
    mix_s,
):
    levels, cols, width = first_ref.shape[1:]
    rows = [
        wide(prev_ref, 0),
        merge_rows(wide(prev_ref, 1), wide(first_ref, 0), mgain_ref[...], mweight_ref[...]),
        wide(upper_ref, 1),
        wide(lower_ref, 0),
        merge_rows(
            wide(first_ref, WIN_ROWS - 1), wide(next_ref, 0), mgain_ref[...], mweight_ref[...]
        ),
        wide(next_ref, 1),
    ]
    for r in range(WIN_ROWS):
        for l in range(levels):
            for w in range(win_s.shape[0]):
                start = (r * levels + l) * WIN_COLS
                win_s[w, start : start + WIN_COLS, :] = rows[r][l, w * WIN_COLS : (w + 1) * WIN_COLS]

    def window(w, carry):
        done = attend(win_s[w], gain_ref[...], qkv_ref, proj_ref, None, qkv_s, mix_s)
        win_s[w] = done
        spread_s[w] = jnp.dot(
            norm(done, sgain_ref[...]), sweight_ref[...], preferred_element_type=jnp.float32
        )
        return carry

    lax.fori_loop(0, win_s.shape[0], window, 0)

    def gathered(ref, r):
        return jnp.stack(
            [
                jnp.concatenate(
                    [
                        ref[w, (r * levels + l) * WIN_COLS : (r * levels + l + 1) * WIN_COLS, :]
                        for w in range(win_s.shape[0])
                    ],
                    axis=0,
                )
                for l in range(levels)
            ]
        )

    to_prev_ref[0] = gathered(win_s, 0).astype(jnp.bfloat16)
    to_next_ref[1] = gathered(win_s, WIN_ROWS - 1).astype(jnp.bfloat16)
    to_prev_ref[1], out_ref[0] = spread_add(
        gathered(spread_s, 1), wide(prev_ref, 1), wide(first_ref, 0)
    )
    out_ref[1], out_ref[2] = spread_add(
        gathered(spread_s, 2), wide(first_ref, 1), wide(first_ref, 2)
    )
    out_ref[3], out_ref[4] = spread_add(
        gathered(spread_s, 3), wide(first_ref, 3), wide(first_ref, 4)
    )
    out_ref[5], to_next_ref[0] = spread_add(
        gathered(spread_s, 4), wide(first_ref, 5), wide(next_ref, 0)
    )
    for r in range(WIN_ROWS):
        for l in range(levels):
            edge_ref[r, l] = out_ref[r, l].astype(jnp.float32)[-HALF_COLS // 2 :].astype(jnp.bfloat16)


def giver_kernel(
    first_ref, prev_ref, next_ref, sgain_ref, sweight_ref, out_ref, edge_ref
):
    levels, cols, width = first_ref.shape[1:]
    both = jnp.concatenate([wide(prev_ref, 1), wide(next_ref, 0)], axis=0)
    spread = jnp.dot(
        norm(both.reshape(2 * levels * cols, width), sgain_ref[...]),
        sweight_ref[...],
        preferred_element_type=jnp.float32,
    ).reshape(2 * levels, cols, 2 * width)
    out_ref[0] = prev_ref[0]
    out_ref[5] = next_ref[1]
    out_ref[1], out_ref[2] = spread_add(spread[:levels], wide(first_ref, 1), wide(first_ref, 2))
    out_ref[3], out_ref[4] = spread_add(spread[levels:], wide(first_ref, 3), wide(first_ref, 4))
    for r in range(WIN_ROWS):
        for l in range(levels):
            edge_ref[r, l] = out_ref[r, l].astype(jnp.float32)[-HALF_COLS // 2 :].astype(jnp.bfloat16)


def last_kernel(
    center,
    place_ref,
    labels_ref,
    joined_ref,
    edge_ref,
    gain_ref,
    qkv_ref,
    proj_ref,
    own_ref,
    main_ref,
    second_ref,
    win_s,
    qkv_s,
    mix_s,
    bias_s,
    row_s,
):
    is_left, first_row = strip_of(place_ref[0], center)
    groups = win_s.shape[1]
    width = groups * LANES
    extra = edge_ref.shape[2]
    for l in range(LEVELS):
        for r in range(WIN_ROWS):
            base = (l * WIN_ROWS + r) * WIN_COLS
            edge = edge_ref[r, l].astype(jnp.float32)
            joined = joined_ref[r, l].astype(jnp.float32)
            for parity in range(2):
                lanes = slice(parity * width, (parity + 1) * width)
                start = base + parity * HALF_COLS
                store(win_s, 0, start, edge[:, lanes])
                store(win_s, 0, start + extra, joined[: HALF_COLS - extra, lanes])
                for w in range(1, win_s.shape[0]):
                    begin = w * HALF_COLS - extra
                    store(win_s, w, start, joined[begin : begin + HALF_COLS, lanes])

    bias_s[...] = make_bias(labels_ref, first_row)

    def window(w, carry):
        done = attend(
            load(win_s, w), gain_ref[...], qkv_ref, proj_ref, bias_s[...], qkv_s, mix_s
        )
        store(win_s, w, 0, done)
        return carry

    lax.fori_loop(0, win_s.shape[0], window, 0)

    def natural(l, r):
        base = (l * WIN_ROWS + r) * WIN_COLS
        for w in range(win_s.shape[0]):
            for parity in range(2):
                start = base + parity * HALF_COLS
                for c in range(groups):
                    row_s[c, pl.ds(w * WIN_COLS + parity, HALF_COLS, stride=2), :] = win_s[
                        w, c, start : start + HALF_COLS, :
                    ]
        return jnp.concatenate([row_s[c] for c in range(groups)], axis=1)

    cut = main_ref.shape[2]

    def finish(own_row, other_row):
        for l in range(LEVELS):
            for r in range(HALF_ROWS):
                own_ref[l, r] = natural(l, own_row + r).astype(jnp.bfloat16)
                other = natural(l, other_row + r)
                main_ref[l, r] = other[:cut].astype(jnp.bfloat16)
                second_ref[l, r] = other[cut:].astype(jnp.bfloat16)

    @pl.when(is_left)
    def _():
        finish(0, HALF_ROWS)

    @pl.when(jnp.logical_not(is_left))
    def _():
        finish(HALF_ROWS, 0)


def bf16(*shape):
    return jax.ShapeDtypeStruct(shape, jnp.bfloat16)


SMEM = pl.BlockSpec(memory_space=pltpu.SMEM)
VMEM = pl.BlockSpec(memory_space=pltpu.VMEM)


def call_first(center, half, place, labels, x, lon, main, second, gain, qkv, proj, mgain, mweight):
    width = x.shape[-1]
    cols = half // 2
    count = half // WIN_COLS + 1
    paired = (LEVELS, cols, 2 * width)
    return pl.pallas_call(
        functools.partial(first_kernel, center, half),
        out_shape=(bf16(WIN_ROWS, *paired), bf16(2, *paired), bf16(2, *paired)),
        in_specs=[SMEM, SMEM] + [VMEM] * 9,
        out_specs=(VMEM, VMEM, VMEM),
        scratch_shapes=[
            pltpu.VMEM((count, width // LANES, TOKENS, LANES), jnp.float32),
            pltpu.VMEM((TOKENS, 3 * width), jnp.bfloat16),
            pltpu.VMEM((TOKENS, width), jnp.bfloat16),
            pltpu.VMEM((TOKENS, TOKENS), jnp.float32),
        ],
        compiler_params=PARAMS,
    )(place, labels, x, lon, main, second, gain, qkv, proj, mgain, mweight)


def call_coarse(first, upper, lower, prev, following, mgain, mweight, gain, qkv, proj, sgain, sweight):
    rows, levels, cols, width = first.shape
    count = cols // WIN_COLS
    paired = (levels, cols, width)
    return pl.pallas_call(
        coarse_kernel,
        out_shape=(
            bf16(rows, *paired),
            bf16(2, *paired),
            bf16(2, *paired),
            bf16(rows, levels, HALF_COLS // 2, width),
        ),
        in_specs=[VMEM] * 12,
        out_specs=(VMEM,) * 4,
        scratch_shapes=[
            pltpu.VMEM((count, TOKENS, width), jnp.float32),
            pltpu.VMEM((count, TOKENS, 2 * width), jnp.float32),
            pltpu.VMEM((TOKENS, 3 * width), jnp.bfloat16),
            pltpu.VMEM((TOKENS, width), jnp.bfloat16),
        ],
        compiler_params=PARAMS,
    )(first, upper, lower, prev, following, mgain, mweight, gain, qkv, proj, sgain, sweight)


def call_giver(first, prev, following, sgain, sweight):
    rows, levels, cols, width = first.shape
    return pl.pallas_call(
        giver_kernel,
        out_shape=(bf16(*first.shape), bf16(rows, levels, HALF_COLS // 2, width)),
        in_specs=[VMEM] * 5,
        out_specs=(VMEM,) * 2,
        compiler_params=PARAMS,
    )(first, prev, following, sgain, sweight)


def call_last(center, place, labels, joined, edge, gain, qkv, proj):
    rows, levels, cols, wide_width = joined.shape
    width = wide_width // 2
    half = 2 * cols
    count = half // WIN_COLS
    return pl.pallas_call(
        functools.partial(last_kernel, center),
        out_shape=(
            bf16(levels, HALF_ROWS, half, width),
            bf16(levels, HALF_ROWS, half - HALF_COLS, width),
            bf16(levels, HALF_ROWS, HALF_COLS, width),
        ),
        in_specs=[SMEM, SMEM] + [VMEM] * 5,
        out_specs=(VMEM,) * 3,
        scratch_shapes=[
            pltpu.VMEM((count, width // LANES, TOKENS, LANES), jnp.float32),
            pltpu.VMEM((TOKENS, 3 * width), jnp.bfloat16),
            pltpu.VMEM((TOKENS, width), jnp.bfloat16),
            pltpu.VMEM((TOKENS, TOKENS), jnp.float32),
            pltpu.VMEM((width // LANES, half, LANES), jnp.float32),
        ],
        compiler_params=PARAMS,
    )(place, labels, joined, edge, gain, qkv, proj)


def send(value, move):
    lats, lons = lax.axis_size("lat"), lax.axis_size("lon")
    pairs = []
    for lat in range(lats):
        for lon in range(lons):
            up, over = move(lat % 2 == 1)
            target = ((lat + up) % lats) * lons + (lon + over) % lons
            pairs.append((lat * lons + lon, target))
    return lax.ppermute(value, ("lat", "lon"), pairs)


def body(
    latent,
    band_labels,
    gain_first,
    qkv_first,
    proj_first,
    merge_gain,
    merge_weight,
    gain_coarse,
    qkv_coarse,
    proj_coarse,
    split_gain,
    split_weight,
    gain_last,
    qkv_last,
    proj_last,
):
    place = lax.axis_index("lat")
    odd = place % 2 == 1
    place = place.reshape(1).astype(jnp.int32)
    cols = latent.shape[2]
    half = cols // 2
    edge = HALF_COLS + half
    cut = cols - edge
    flat = lambda gain: gain.reshape(1, -1)

    for_prev = latent[:, :HALF_ROWS]
    for_next = latent[:, HALF_ROWS:]
    prev_main = for_prev[:, :, HALF_COLS : HALF_COLS + cut]
    prev_second = for_prev[:, :, HALF_COLS + cut : edge + WIN_COLS]
    next_main = for_next[:, :, edge:]
    next_second = for_next[:, :, : WIN_COLS + HALF_COLS]
    lon = send(for_prev[:, :, : WIN_COLS + HALF_COLS], lambda is_odd: (0, -1))
    x_main = send(jnp.where(odd, prev_main, next_main), lambda is_odd: (-1, 0) if is_odd else (1, 0))
    x_second = send(
        jnp.where(odd, prev_second, next_second), lambda is_odd: (-1, 0) if is_odd else (1, -1)
    )
    c_main = send(jnp.where(odd, next_main, prev_main), lambda is_odd: (1, 0) if is_odd else (-1, 0))
    c_second = send(
        jnp.where(odd, next_second, prev_second), lambda is_odd: (1, -1) if is_odd else (-1, 0)
    )

    weights = (flat(gain_first), qkv_first, proj_first, flat(merge_gain), merge_weight)
    first_x, upper_x, lower_x = call_first(
        False, half, place, band_labels, latent, lon, x_main, x_second, *weights
    )
    from_next = send(upper_x, lambda is_odd: (-1, 0))
    from_prev = send(lower_x, lambda is_odd: (1, 0))
    first_c, upper_c, lower_c = call_first(
        True, half, place, band_labels, latent, lon, c_main, c_second, *weights
    )
    joined_c, to_prev, to_next, edge_c = call_coarse(
        first_c,
        upper_c,
        lower_c,
        from_prev,
        from_next,
        flat(merge_gain),
        merge_weight,
        flat(gain_coarse),
        qkv_coarse,
        proj_coarse,
        flat(split_gain),
        split_weight,
    )
    edge_c = send(edge_c, lambda is_odd: (1, 0) if is_odd else (-1, 1))
    back_next = send(to_prev, lambda is_odd: (-1, 0))
    back_prev = send(to_next, lambda is_odd: (1, 0))
    weights = (flat(gain_last), qkv_last, proj_last)
    own_c, main_c, second_c = call_last(True, place, band_labels, joined_c, edge_c, *weights)
    main_c = send(main_c, lambda is_odd: (1, 0) if is_odd else (-1, 0))
    second_c = send(second_c, lambda is_odd: (1, 0) if is_odd else (-1, 1))
    joined_x, edge_x = call_giver(first_x, back_prev, back_next, flat(split_gain), split_weight)
    edge_x = send(edge_x, lambda is_odd: (-1, 1) if is_odd else (1, 0))
    own_x, main_x, second_x = call_last(False, place, band_labels, joined_x, edge_x, *weights)
    main_x = send(main_x, lambda is_odd: (-1, 0) if is_odd else (1, 0))
    second_x = send(second_x, lambda is_odd: (-1, 1) if is_odd else (1, 0))

    own_left = jnp.where(odd, own_c, own_x)
    own_right = jnp.where(odd, own_x, own_c)
    lon_back = send(own_right[:, :, cut:], lambda is_odd: (0, 1))
    left_main, left_second = jnp.where(odd, main_x, main_c), jnp.where(odd, second_x, second_c)
    right_main, right_second = jnp.where(odd, main_c, main_x), jnp.where(odd, second_c, second_x)
    top = jnp.concatenate([lon_back, left_main, left_second, own_right[:, :, :cut]], axis=2)
    bottom = jnp.concatenate([right_second, own_left, right_main], axis=2)
    return jnp.concatenate([top, bottom], axis=1)


def solution(mesh):
    return jax.shard_map(
        body,
        mesh=mesh,
        in_specs=(P("rep", "lat", "lon", None),) + (P(),) * 14,
        out_specs=P("rep", "lat", "lon", None),
        check_vma=False,
    )
```

time: 560 us -> 163 us (0.29); the launches traced: 550 us -> 162 us
  local copies, waits for them, and re-layouts: 217 us -> 5.26 us
  matrix products: 114 us -> 0 us
  waiting for transfers between devices: 163 us -> 54 us
  Pallas kernels: 0 us -> 74.7 us
  other arithmetic: 42.1 us -> 5.65 us
  starting transfers between devices: 12.4 us -> 22.6 us
    ppermute x13 -> x16, waiting for transfers between devices: 163 us -> 54 us  [send(): return lax.ppermute(value, ('lat', 'lon'), pairs)]
    dot_general x17 -> x0, matrix products: 98.3 us -> none  [the longest x3 27.8 us: attend(): jnp.einsum('whqk,wkhd->wqhd', weights, paired[:, :, 1], preferred_element...]
    pallas_call x0 -> x6, Pallas kernels: none -> 74.7 us  [the longest x2 30.5 us: call_first(): pl.pallas_call(functools.partial(first_kernel, center, half), out_shape=(...]
    reshape x11 -> x0, local copies, waits for them, and re-layouts: 64.1 us -> none  [the longest x3 30.9 us: attend(): paired.astype(jnp.bfloat16).reshape(count, key_tokens, 2, heads, HEAD_DIM)]
    slice x16 -> x1, local copies, waits for them, and re-layouts: 45.5 us -> 0.02 us  [body(): lon_back = send(own_right[:, :, cut:], lambda is_odd: (0, 1))]
    dot_general x7 -> x0, local copies, waits for them, and re-layouts: 33.8 us -> none  [the longest x6 27.1 us: attend(): jnp.dot(mixed, proj_weight, preferred_element_type=jnp.float32)]
    unnamed x44 -> x22, local copies, waits for them, and re-layouts: 32.5 us -> 5.24 us
    transpose x8 -> x0, local copies, waits for them, and re-layouts: 18.4 us -> none  [the longest x3 7.78 us: from_windows(): blocks.reshape(count, levels, rows, WIN_COLS, width)]
  transfers between devices with their start and end apart: 13 -> 16, of which waited for: 12 -> 6; matrix products, arithmetic and copies ran while one was open for 2% -> 2% of each run, Pallas kernels for 0% -> 34%
where the time goes in v1:
time: 163 us; the launch traced here: 162 us
  Pallas kernels  74.7 us (46%)
  waiting for transfers between devices  54 us (33%)
  starting transfers between devices  22.6 us (14%)
  other arithmetic  5.65 us (3%)
  local copies, waits for them, and re-layouts  5.26 us (3%)
    ppermute x16, waiting for transfers between devices, send(): return lax.ppermute(value, ('lat', 'lon'), pairs)  54 us
    pallas_call x2, Pallas kernels, call_first(): pl.pallas_call(functools.partial(first_kernel, center, half), out_shape=(...  30.5 us
    ppermute x16, starting transfers between devices, send(): return lax.ppermute(value, ('lat', 'lon'), pairs)  22.6 us
    pallas_call x2, Pallas kernels, call_last(): pl.pallas_call(functools.partial(last_kernel, center), out_shape=(bf16(le...  19.8 us
    pallas_call x1, Pallas kernels, call_coarse(): pl.pallas_call(coarse_kernel, out_shape=(bf16(rows, *paired), bf16(2, *pa...  19.7 us
    unnamed x22, local copies, waits for them, and re-layouts  5.24 us
    pallas_call x1, Pallas kernels, call_giver(): pl.pallas_call(giver_kernel, out_shape=(bf16(*first.shape), bf16(rows, le...  4.66 us
  transfers between devices with their start and end apart: 16, of which 6 were waited for; matrix products, arithmetic and copies ran while one was open for 2% of the time, Pallas kernels for 34%

profile of v1, /device:TPU:0, one launch (start us, length us, event | category | flops | bytes accessed | tf_op | source)
XLA Modules:
  0.0 162.4 jit_solution(9916219828997982858)
XLA Ops:
  0.0 1.4 broadcast_select_fusion.3
  1.4 3.1 %collective-permute-start.1 = (bf16[3,3,42,512]{3,2,1,0:T(8,128)(2,1)S(1)}, bf16[3,3,42,512]{3,2,1,0:T(8,128)(2,1)S(1)}, u32[]{:S(2)}, u32[]{:S(2)}) collective-permute-start(bf16[3,3,42,512]{3,2,1,0:T(8,128)(2,1)S(1)} %get-tuple-element.44), channel_id=1, source_target_pairs={{0,8},{2,10},{4,12},{6,14},{8,0},{10,2},{12,4},{14,6},{16,24},{18,... | collective-permute-start | bytes 1161224 | tf_op jit(solution)/shard_map/ppermute | solution.py:493
  4.5 1.2 broadcast_select_fusion.7
  6.3 1.1 collective-permute-start
  7.4 2.8 %collective-permute-start.3 = (bf16[3,3,42,512]{3,2,1,0:T(8,128)(2,1)S(1)}, bf16[3,3,42,512]{3,2,1,0:T(8,128)(2,1)S(1)}, u32[]{:S(2)}, u32[]{:S(2)}) collective-permute-start(bf16[3,3,42,512]{3,2,1,0:T(8,128)(2,1)S(1)} %get-tuple-element.45), channel_id=1, source_target_pairs={{0,24},{2,26},{4,28},{6,30},{8,16},{10,18},{12,20},{14,22},{16,8},... | collective-permute-start | bytes 1161224 | tf_op jit(solution)/shard_map/ppermute | solution.py:493
  10.2 9.6 %collective-permute-done.2.second_ref = bf16[3,3,18,512]{3,2,1,0:T(8,128)(2,1)S(1)} collective-permute-done((bf16[3,3,18,512]{3,2,1,0:T(8,128)(2,1)S(1)}, bf16[3,3,18,512]{3,2,1,0:T(8,128)(2,1)S(1)}, u32[]{:S(2)}, u32[]{:S(2)}) %collective-permute-start.2) | collective-permute-done | bytes 165920 | tf_op jit(solution)/shard_map/ppermute | solution.py:493
  19.8 0.7 copy-done.7
  20.8 15.2 %shard_map.145 = (bf16[6,3,24,1024]{3,2,1,0:T(8,128)(2,1)}, bf16[2,3,24,1024]{3,2,1,0:T(8,128)(2,1)}, bf16[2,3,24,1024]{3,2,1,0:T(8,128)(2,1)}) custom-call(s32[1]{0:T(128)} %bitcast.place_ref, s32[24]{0:T(128)} %labels_ref.7, bf16[3,6,96,512]{3,2,1,0:T(8,128)(2,1)} %x_ref.3, bf16[3,3,18,512]{3,2,1,0:T(8,128)(2,1)} %copy-done, ...), custom_call_target="tpu_custom_call" | custom-call | tf_op jit(solution)/shard_map/pallas_call | solution.py:410
  36.1 3.7 %collective-permute-start.6 = (bf16[2,3,24,1024]{3,2,1,0:T(8,128)(2,1)}, bf16[2,3,24,1024]{3,2,1,0:T(8,128)(2,1)S(1)}, u32[]{:S(2)}, u32[]{:S(2)}) collective-permute-start(bf16[2,3,24,1024]{3,2,1,0:T(8,128)(2,1)} %get-tuple-element.28), channel_id=1, source_target_pairs={{0,24},{2,26},{4,28},{6,30},{8,0},{10,2},{12,4},{14,6},{16,8},{18,... | collective-permute-start | bytes 884744 | tf_op jit(solution)/shard_map/ppermute | solution.py:493
  39.8 1.1 collective-permute-start.4
  40.9 20.9 %collective-permute-done.4.second_ref = bf16[3,3,18,512]{3,2,1,0:T(8,128)(2,1)S(1)} collective-permute-done((bf16[3,3,18,512]{3,2,1,0:T(8,128)(2,1)S(1)}, bf16[3,3,18,512]{3,2,1,0:T(8,128)(2,1)S(1)}, u32[]{:S(2)}, u32[]{:S(2)}) %collective-permute-start.4) | collective-permute-done | bytes 165920 | tf_op jit(solution)/shard_map/ppermute | solution.py:493
  61.8 0.7 copy-done.8
  62.5 0.8 copy-done.1
  63.2 15.3 %shard_map.146 = (bf16[6,3,24,1024]{3,2,1,0:T(8,128)(2,1)}, bf16[2,3,24,1024]{3,2,1,0:T(8,128)(2,1)}, bf16[2,3,24,1024]{3,2,1,0:T(8,128)(2,1)}) custom-call(s32[1]{0:T(128)} %bitcast.place_ref, s32[24]{0:T(128)} %labels_ref.7, bf16[3,6,96,512]{3,2,1,0:T(8,128)(2,1)} %x_ref.3, bf16[3,3,18,512]{3,2,1,0:T(8,128)(2,1)} %copy-done, ...), custom_call_target="tpu_custom_call" | custom-call | tf_op jit(solution)/shard_map/pallas_call | solution.py:410
  78.6 0.7 copy-done.5
  79.4 19.7 %shard_map.147 = (bf16[6,3,24,1024]{3,2,1,0:T(8,128)(2,1)}, bf16[2,3,24,1024]{3,2,1,0:T(8,128)(2,1)}, bf16[2,3,24,1024]{3,2,1,0:T(8,128)(2,1)}, bf16[6,3,3,1024]{3,2,1,0:T(4,128)(2,1)}) custom-call(bf16[6,3,24,1024]{3,2,1,0:T(8,128)(2,1)} %get-tuple-element.24.first_ref, bf16[2,3,24,1024]{3,2,1,0:T(8,128)(2,1)} %get-tuple-element.25.upper_ref, ...), custom_call_target="tpu_custom_call" | custom-call | tf_op jit(solution)/shard_map/pallas_call | solution.py:429
  99.2 3.8 %collective-permute-start.8 = (bf16[2,3,24,1024]{3,2,1,0:T(8,128)(2,1)}, bf16[2,3,24,1024]{3,2,1,0:T(8,128)(2,1)S(1)}, u32[]{:S(2)}, u32[]{:S(2)}) collective-permute-start(bf16[2,3,24,1024]{3,2,1,0:T(8,128)(2,1)} %get-tuple-element.30), channel_id=1, source_target_pairs={{0,24},{2,26},{4,28},{6,30},{8,0},{10,2},{12,4},{14,6},{16,8},{18,... | collective-permute-start | bytes 884744 | tf_op jit(solution)/shard_map/ppermute | solution.py:493
  103.0 8.2 %collective-permute-done.7.prev_ref = bf16[2,3,24,1024]{3,2,1,0:T(8,128)(2,1)S(1)} collective-permute-done((bf16[2,3,24,1024]{3,2,1,0:T(8,128)(2,1)}, bf16[2,3,24,1024]{3,2,1,0:T(8,128)(2,1)S(1)}, u32[]{:S(2)}, u32[]{:S(2)}) %collective-permute-start.7) | collective-permute-done | bytes 294944 | tf_op jit(solution)/shard_map/ppermute | solution.py:493
  111.1 4.7 %collective-permute-done.8.next_ref = bf16[2,3,24,1024]{3,2,1,0:T(8,128)(2,1)S(1)} collective-permute-done((bf16[2,3,24,1024]{3,2,1,0:T(8,128)(2,1)}, bf16[2,3,24,1024]{3,2,1,0:T(8,128)(2,1)S(1)}, u32[]{:S(2)}, u32[]{:S(2)}) %collective-permute-start.8) | collective-permute-done | bytes 294944 | tf_op jit(solution)/shard_map/ppermute | solution.py:493
  115.9 0.7 copy-done.4
  116.6 4.7 %shard_map.148 = (bf16[6,3,24,1024]{3,2,1,0:T(8,128)(2,1)}, bf16[6,3,3,1024]{3,2,1,0:T(4,128)(2,1)}) custom-call(bf16[6,3,24,1024]{3,2,1,0:T(8,128)(2,1)} %get-tuple-element.23.first_ref, bf16[2,3,24,1024]{3,2,1,0:T(8,128)(2,1)} %copy-done.3, bf16[2,3,24,1024]{3,2,1,0:T(8,128)(2,1)} %copy-done.4, f32[1,1024]{1,0:T(1,128)} %bitcast.12, ...), custom_call_target="tpu_custom_call" | custom-call | tf_op jit(solution)/shard_map/pallas_call | solution.py:451
  121.9 0.7 copy-done.10
  122.5 9.9 %shard_map.150 = (bf16[3,3,48,512]{3,2,1,0:T(8,128)(2,1)}, bf16[3,3,42,512]{3,2,1,0:T(8,128)(2,1)}, bf16[3,3,6,512]{3,2,1,0:T(8,128)(2,1)}) custom-call(s32[1]{0:T(128)} %bitcast.place_ref, s32[24]{0:T(128)} %labels_ref.7, bf16[6,3,24,1024]{3,2,1,0:T(8,128)(2,1)} %get-tuple-element.34.joined_ref, bf16[6,3,3,1024]{3,2,1,0:T(4,128)(2,1)} %copy-done.10, ...), custom_call_target="tpu_custom_call" | custom-call | tf_op jit(solution)/shard_map/pallas_call | solution.py:465
  132.5 2.0 %collective-permute-start.15 = (bf16[3,3,6,512]{3,2,1,0:T(8,128)(2,1)}, bf16[3,3,6,512]{3,2,1,0:T(8,128)(2,1)S(1)}, u32[]{:S(2)}, u32[]{:S(2)}) collective-permute-start(bf16[3,3,6,512]{3,2,1,0:T(8,128)(2,1)} %get-tuple-element.40), channel_id=1, source_target_pairs={{0,26},{2,28},{4,30},{6,24},{8,16},{10,18},{12,20},{14,22},{16,10}... | collective-permute-start | bytes 165896 | tf_op jit(solution)/shard_map/ppermute | solution.py:493
  134.5 2.8 %collective-permute-start.13 = (bf16[3,3,42,512]{3,2,1,0:T(8,128)(2,1)}, bf16[3,3,42,512]{3,2,1,0:T(8,128)(2,1)S(1)}, u32[]{:S(2)}, u32[]{:S(2)}) collective-permute-start(bf16[3,3,42,512]{3,2,1,0:T(8,128)(2,1)} %get-tuple-element.38), channel_id=1, source_target_pairs={{0,24},{2,26},{4,28},{6,30},{8,16},{10,18},{12,20},{14,22},{16,8},... | collective-permute-start | bytes 1161224 | tf_op jit(solution)/shard_map/ppermute | solution.py:493
  137.3 0.7 copy-done.9
  138.0 9.9 %shard_map.149 = (bf16[3,3,48,512]{3,2,1,0:T(8,128)(2,1)}, bf16[3,3,42,512]{3,2,1,0:T(8,128)(2,1)}, bf16[3,3,6,512]{3,2,1,0:T(8,128)(2,1)}) custom-call(s32[1]{0:T(128)} %bitcast.place_ref, s32[24]{0:T(128)} %labels_ref.7, bf16[6,3,24,1024]{3,2,1,0:T(8,128)(2,1)} %get-tuple-element.31.joined_ref, bf16[6,3,3,1024]{3,2,1,0:T(4,128)(2,1)} %copy-done.9, ...), custom_call_target="tpu_custom_call" | custom-call | tf_op jit(solution)/shard_map/pallas_call | solution.py:465
  147.9 1.2 broadcast_select_fusion.5
  149.1 0.8 collective-permute-start.11
  149.9 3.3 %collective-permute-done.14 = bf16[3,3,6,512]{3,2,1,0:T(8,128)(2,1)S(1)} collective-permute-done((bf16[3,3,6,512]{3,2,1,0:T(8,128)(2,1)}, bf16[3,3,6,512]{3,2,1,0:T(8,128)(2,1)S(1)}, u32[]{:S(2)}, u32[]{:S(2)}) %collective-permute-start.14) | collective-permute-done | bytes 55328 | tf_op jit(solution)/shard_map/ppermute | solution.py:493
  153.3 7.3 %collective-permute-done.12 = bf16[3,3,42,512]{3,2,1,0:T(8,128)(2,1)S(1)} collective-permute-done((bf16[3,3,42,512]{3,2,1,0:T(8,128)(2,1)}, bf16[3,3,42,512]{3,2,1,0:T(8,128)(2,1)S(1)}, u32[]{:S(2)}, u32[]{:S(2)}) %collective-permute-start.12) | collective-permute-done | bytes 387104 | tf_op jit(solution)/shard_map/ppermute | solution.py:493
  160.6 1.8 %maximum_maximum_fusion = bf16[3,6,96,512]{3,2,1,0:T(8,128)(2,1)} fusion(bf16[3,3,42,512]{3,2,1,0:T(8,128)(2,1)S(1)} %get-tuple-element.47, bf16[3,3,48,512]{3,2,1,0:T(8,128)(2,1)S(1)} %get-tuple-element.49, bf16[3,3,6,512]{3,2,1,0:T(8,128)(2,1)S(1)} %get-tuple-element.51, bf16[3,3,42,512]{3,2,1,0:T(8,128)(2,1)S(1)} %bitcast.7, ...), kind=kLoop, calls=%fused_computation | loop fusion | flops 12386304 | bytes 3538944 | tf_op jit(solution)/shard_map/concatenate | solution.py:581
  (35 shorter events, 2.0 us)
Async XLA Ops:
  1.4 18.4 %collective-permute-start.1 = (bf16[3,3,42,512]{3,2,1,0:T(8,128)(2,1)S(1)}, bf16[3,3,42,512]{3,2,1,0:T(8,128)(2,1)S(1)}, u32[]{:S(2)}, u32[]{:S(2)}) collective-permute-start(bf16[3,3,42,512]{3,2,1,0:T(8,128)(2,1)S(1)} %get-tuple-element.44), channel_id=1, source_target_pairs={{0,8},{2,10},{4,12},{6,14},{8,0},{10,2},{12,4},{14,6},{16,24},{18,... | collective-permute-start | bytes 1161224 | tf_op jit(solution)/shard_map/ppermute | solution.py:493
  5.7 14.1 %collective-permute-start.2 = (bf16[3,3,18,512]{3,2,1,0:T(8,128)(2,1)S(1)}, bf16[3,3,18,512]{3,2,1,0:T(8,128)(2,1)S(1)}, u32[]{:S(2)}, u32[]{:S(2)}) collective-permute-start(bf16[3,3,18,512]{3,2,1,0:T(8,128)(2,1)S(1)} %get-tuple-element.41), channel_id=1, source_target_pairs={{0,14},{2,8},{4,10},{6,12},{8,0},{10,2},{12,4},{14,6},{16,30},{18,... | collective-permute-start | bytes 497672 | tf_op jit(solution)/shard_map/ppermute | solution.py:493
  6.3 13.5 %collective-permute-start = (bf16[3,3,18,512]{3,2,1,0:T(8,128)(2,1)S(1)}, bf16[3,3,18,512]{3,2,1,0:T(8,128)(2,1)S(1)}, u32[]{:S(2)}, u32[]{:S(2)}) collective-permute-start(bf16[3,3,18,512]{3,2,1,0:T(8,128)(2,1)S(1)} %get-tuple-element.42), channel_id=1, source_target_pairs={{0,6},{2,0},{4,2},{6,4},{8,14},{10,8},{12,10},{14,12},{16,22},{18,... | collective-permute-start | bytes 497672 | tf_op jit(solution)/shard_map/ppermute | solution.py:493
  7.4 54.4 %collective-permute-start.3 = (bf16[3,3,42,512]{3,2,1,0:T(8,128)(2,1)S(1)}, bf16[3,3,42,512]{3,2,1,0:T(8,128)(2,1)S(1)}, u32[]{:S(2)}, u32[]{:S(2)}) collective-permute-start(bf16[3,3,42,512]{3,2,1,0:T(8,128)(2,1)S(1)} %get-tuple-element.45), channel_id=1, source_target_pairs={{0,24},{2,26},{4,28},{6,30},{8,16},{10,18},{12,20},{14,22},{16,8},... | collective-permute-start | bytes 1161224 | tf_op jit(solution)/shard_map/ppermute | solution.py:493
  19.8 0.7 copy-start.7
  19.8 0.8 copy-start
  19.8 1.0 copy-start.2
  35.9 42.7 %collective-permute-start.5 = (bf16[2,3,24,1024]{3,2,1,0:T(8,128)(2,1)}, bf16[2,3,24,1024]{3,2,1,0:T(8,128)(2,1)S(1)}, u32[]{:S(2)}, u32[]{:S(2)}) collective-permute-start(bf16[2,3,24,1024]{3,2,1,0:T(8,128)(2,1)} %get-tuple-element.27), channel_id=1, source_target_pairs={{0,8},{2,10},{4,12},{6,14},{8,16},{10,18},{12,20},{14,22},{16,24},... | collective-permute-start | bytes 884744 | tf_op jit(solution)/shard_map/ppermute | solution.py:493
  36.1 42.5 %collective-permute-start.6 = (bf16[2,3,24,1024]{3,2,1,0:T(8,128)(2,1)}, bf16[2,3,24,1024]{3,2,1,0:T(8,128)(2,1)S(1)}, u32[]{:S(2)}, u32[]{:S(2)}) collective-permute-start(bf16[2,3,24,1024]{3,2,1,0:T(8,128)(2,1)} %get-tuple-element.28), channel_id=1, source_target_pairs={{0,24},{2,26},{4,28},{6,30},{8,0},{10,2},{12,4},{14,6},{16,8},{18,... | collective-permute-start | bytes 884744 | tf_op jit(solution)/shard_map/ppermute | solution.py:493
  39.8 22.0 %collective-permute-start.4 = (bf16[3,3,18,512]{3,2,1,0:T(8,128)(2,1)S(1)}, bf16[3,3,18,512]{3,2,1,0:T(8,128)(2,1)S(1)}, u32[]{:S(2)}, u32[]{:S(2)}) collective-permute-start(bf16[3,3,18,512]{3,2,1,0:T(8,128)(2,1)S(1)} %get-tuple-element.43), channel_id=1, source_target_pairs={{0,24},{2,26},{4,28},{6,30},{8,22},{10,16},{12,18},{14,20},{16,8},... | collective-permute-start | bytes 497672 | tf_op jit(solution)/shard_map/ppermute | solution.py:493
  61.8 0.7 copy-start.8
  62.5 0.8 copy-start.1
  78.6 0.7 copy-start.5
  78.6 0.8 copy-start.6
  99.1 12.0 %collective-permute-start.7 = (bf16[2,3,24,1024]{3,2,1,0:T(8,128)(2,1)}, bf16[2,3,24,1024]{3,2,1,0:T(8,128)(2,1)S(1)}, u32[]{:S(2)}, u32[]{:S(2)}) collective-permute-start(bf16[2,3,24,1024]{3,2,1,0:T(8,128)(2,1)} %get-tuple-element.29), channel_id=1, source_target_pairs={{0,8},{2,10},{4,12},{6,14},{8,16},{10,18},{12,20},{14,22},{16,24},... | collective-permute-start | bytes 884744 | tf_op jit(solution)/shard_map/ppermute | solution.py:493
  99.2 16.7 %collective-permute-start.8 = (bf16[2,3,24,1024]{3,2,1,0:T(8,128)(2,1)}, bf16[2,3,24,1024]{3,2,1,0:T(8,128)(2,1)S(1)}, u32[]{:S(2)}, u32[]{:S(2)}) collective-permute-start(bf16[2,3,24,1024]{3,2,1,0:T(8,128)(2,1)} %get-tuple-element.30), channel_id=1, source_target_pairs={{0,24},{2,26},{4,28},{6,30},{8,0},{10,2},{12,4},{14,6},{16,8},{18,... | collective-permute-start | bytes 884744 | tf_op jit(solution)/shard_map/ppermute | solution.py:493
  103.0 18.9 %collective-permute-start.10 = (bf16[6,3,3,1024]{3,2,1,0:T(4,128)(2,1)}, bf16[6,3,3,1024]{3,2,1,0:T(4,128)(2,1)S(1)}, u32[]{:S(2)}, u32[]{:S(2)}) collective-permute-start(bf16[6,3,3,1024]{3,2,1,0:T(4,128)(2,1)} %get-tuple-element.35), channel_id=1, source_target_pairs={{0,26},{2,28},{4,30},{6,24},{8,16},{10,18},{12,20},{14,22},{16,10}... | collective-permute-start | bytes 331784 | tf_op jit(solution)/shard_map/ppermute | solution.py:493
  111.1 4.7 %copy-start.3 = (bf16[2,3,24,1024]{3,2,1,0:T(8,128)(2,1)}, bf16[2,3,24,1024]{3,2,1,0:T(8,128)(2,1)S(1)}, u32[]{:S(2)}) copy-start(bf16[2,3,24,1024]{3,2,1,0:T(8,128)(2,1)S(1)} %collective-permute-done.7.prev_ref) | copy-start | bytes 884740
  115.9 0.7 copy-start.4
  121.2 16.1 %collective-permute-start.9 = (bf16[6,3,3,1024]{3,2,1,0:T(4,128)(2,1)}, bf16[6,3,3,1024]{3,2,1,0:T(4,128)(2,1)S(1)}, u32[]{:S(2)}, u32[]{:S(2)}) collective-permute-start(bf16[6,3,3,1024]{3,2,1,0:T(4,128)(2,1)} %get-tuple-element.32), channel_id=1, source_target_pairs={{0,8},{2,10},{4,12},{6,14},{8,2},{10,4},{12,6},{14,0},{16,24},{18,... | collective-permute-start | bytes 331784 | tf_op jit(solution)/shard_map/ppermute | solution.py:493
  121.9 0.7 copy-start.10
  132.5 17.5 %collective-permute-start.15 = (bf16[3,3,6,512]{3,2,1,0:T(8,128)(2,1)}, bf16[3,3,6,512]{3,2,1,0:T(8,128)(2,1)S(1)}, u32[]{:S(2)}, u32[]{:S(2)}) collective-permute-start(bf16[3,3,6,512]{3,2,1,0:T(8,128)(2,1)} %get-tuple-element.40), channel_id=1, source_target_pairs={{0,26},{2,28},{4,30},{6,24},{8,16},{10,18},{12,20},{14,22},{16,10}... | collective-permute-start | bytes 165896 | tf_op jit(solution)/shard_map/ppermute | solution.py:493
  134.5 18.8 %collective-permute-start.13 = (bf16[3,3,42,512]{3,2,1,0:T(8,128)(2,1)}, bf16[3,3,42,512]{3,2,1,0:T(8,128)(2,1)S(1)}, u32[]{:S(2)}, u32[]{:S(2)}) collective-permute-start(bf16[3,3,42,512]{3,2,1,0:T(8,128)(2,1)} %get-tuple-element.38), channel_id=1, source_target_pairs={{0,24},{2,26},{4,28},{6,30},{8,16},{10,18},{12,20},{14,22},{16,8},... | collective-permute-start | bytes 1161224 | tf_op jit(solution)/shard_map/ppermute | solution.py:493
  137.3 0.7 copy-start.9
  147.9 5.4 %collective-permute-start.14 = (bf16[3,3,6,512]{3,2,1,0:T(8,128)(2,1)}, bf16[3,3,6,512]{3,2,1,0:T(8,128)(2,1)S(1)}, u32[]{:S(2)}, u32[]{:S(2)}) collective-permute-start(bf16[3,3,6,512]{3,2,1,0:T(8,128)(2,1)} %get-tuple-element.39), channel_id=1, source_target_pairs={{0,8},{2,10},{4,12},{6,14},{8,2},{10,4},{12,6},{14,0},{16,24},{18,... | collective-permute-start | bytes 165896 | tf_op jit(solution)/shard_map/ppermute | solution.py:493
  147.9 12.7 %collective-permute-start.12 = (bf16[3,3,42,512]{3,2,1,0:T(8,128)(2,1)}, bf16[3,3,42,512]{3,2,1,0:T(8,128)(2,1)S(1)}, u32[]{:S(2)}, u32[]{:S(2)}) collective-permute-start(bf16[3,3,42,512]{3,2,1,0:T(8,128)(2,1)} %get-tuple-element.37), channel_id=1, source_target_pairs={{0,8},{2,10},{4,12},{6,14},{8,0},{10,2},{12,4},{14,6},{16,24},{18,... | collective-permute-start | bytes 1161224 | tf_op jit(solution)/shard_map/ppermute | solution.py:493
  149.1 11.5 %collective-permute-start.11 = (bf16[3,3,6,512]{3,2,1,0:T(8,128)(2,1)S(1)}, bf16[3,3,6,512]{3,2,1,0:T(8,128)(2,1)S(1)}, u32[]{:S(2)}, u32[]{:S(2)}) collective-permute-start(bf16[3,3,6,512]{3,2,1,0:T(8,128)(2,1)S(1)} %slice.35), channel_id=1, source_target_pairs={{0,2},{2,4},{4,6},{6,0},{8,10},{10,12},{12,14},{14,8},{16,18},{18,... | collective-permute-start | bytes 165896 | tf_op jit(solution)/shard_map/ppermute | solution.py:493

commit v2 on v1

--- a/solution.py
+++ b/solution.py
@@ -15,8 +15,9 @@
 HALF_COLS = WIN_COLS // 2
 TOKENS = LEVELS * WIN_ROWS * WIN_COLS
 LANES = 128
+AT_ONCE = 2
 SCALE = HEAD_DIM**-0.5 * math.log2(math.e)
-PARAMS = pltpu.CompilerParams(vmem_limit_bytes=60 * 1024 * 1024)
+PARAMS = pltpu.CompilerParams(vmem_limit_bytes=28 * 1024 * 1024)
 
 
 def norm(wide, gain):
@@ -30,43 +31,57 @@
     return value.astype(jnp.bfloat16).astype(jnp.float32)
 
 
-def attend(x, gain, qkv_ref, proj_ref, bias, qkv_s, mix_s):
-    width = x.shape[1]
-    normed = norm(x, gain)
-    for third in range(3):
-        part = jnp.dot(
-            normed,
-            qkv_ref[:, third * width : (third + 1) * width],
-            preferred_element_type=jnp.float32,
-        )
-        qkv_s[:, third * width : (third + 1) * width] = part.astype(jnp.bfloat16)
+def attend(windows, gain, qkv_ref, proj_ref, bias, qkv_s, mix_s):
+    width = windows[0].shape[1]
     pair = 2 * HEAD_DIM
+    for i, x in enumerate(windows):
+        normed = norm(x, gain)
+        for third in range(3):
+            lanes = slice(third * width, (third + 1) * width)
+            part = jnp.dot(normed, qkv_ref[:, lanes], preferred_element_type=jnp.float32)
+            qkv_s[i, :, lanes] = part.astype(jnp.bfloat16)
     low = lax.broadcasted_iota(jnp.int32, (TOKENS, pair), 1) < HEAD_DIM
     ones = jnp.ones((TOKENS, pair), jnp.bfloat16)
     zeros = jnp.zeros((TOKENS, pair), jnp.bfloat16)
-    for j in range(width // pair):
-        q = qkv_s[:, j * pair : (j + 1) * pair]
-        k = qkv_s[:, width + j * pair : width + (j + 1) * pair]
-        v = qkv_s[:, 2 * width + j * pair : 2 * width + (j + 1) * pair]
-        summed = jnp.concatenate([v, ones], axis=1)
-        parts = []
-        for keep in (low, ~low):
-            s = lax.dot_general(
-                q,
-                jnp.where(keep, k, zeros),
-                (((1,), (1,)), ((), ())),
-                preferred_element_type=jnp.float32,
-            )
-            s = s * SCALE
-            if bias is not None:
-                s = s + bias
-            p = jnp.exp2(s - jnp.max(s, axis=-1, keepdims=True)).astype(jnp.bfloat16)
-            r = jnp.dot(p, summed, preferred_element_type=jnp.float32)
-            parts.append(r[:, :pair] / r[:, pair:])
-        mix_s[:, j * pair : (j + 1) * pair] = jnp.where(low, parts[0], parts[1]).astype(
-            jnp.bfloat16
+    steps = [
+        (i, j, keep)
+        for j in range(width // pair)
+        for i in range(len(windows))
+        for keep in (low, ~low)
+    ]
+
+    def scored(step):
+        i, j, keep = step
+        q = qkv_s[i, :, j * pair : (j + 1) * pair]
+        k = qkv_s[i, :, width + j * pair : width + (j + 1) * pair]
+        return lax.dot_general(
+            q,
+            jnp.where(keep, k, zeros),
+            (((1,), (1,)), ((), ())),
+            preferred_element_type=jnp.float32,
         )
-    return rounded(x + jnp.dot(mix_s[...], proj_ref[...], preferred_element_type=jnp.float32))
+
+    first = None
+    ahead = scored(steps[0])
+    for n, (i, j, keep) in enumerate(steps):
+        s = ahead * SCALE
+        if n + 1 < len(steps):
+            ahead = scored(steps[n + 1])
+        if bias is not None:
+            s = s + bias
+        p = jnp.exp2(s - jnp.max(s, axis=-1, keepdims=True)).astype(jnp.bfloat16)
+        v = qkv_s[i, :, 2 * width + j * pair : 2 * width + (j + 1) * pair]
+        r = jnp.dot(p, jnp.concatenate([v, ones], axis=1), preferred_element_type=jnp.float32)
+        if n % 2 == 0:
+            first = r
+        else:
+            mixed = jnp.where(low, first[:, :pair], r[:, :pair])
+            total = jnp.where(low, first[:, pair:], r[:, pair:])
+            mix_s[i, :, j * pair : (j + 1) * pair] = (mixed / total).astype(jnp.bfloat16)
+    return [
+        rounded(x + jnp.dot(mix_s[i], proj_ref[...], preferred_element_type=jnp.float32))
+        for i, x in enumerate(windows)
+    ]
 
 
 def row_of(dim):
@@ -99,6 +114,24 @@
 def store(win_s, w, start, value):
     for c in range(win_s.shape[1]):
         win_s[w, c, start : start + value.shape[0], :] = value[:, c * LANES : (c + 1) * LANES]
+
+
+def attend_all(win_s, gain_ref, qkv_ref, proj_ref, bias_s, qkv_s, mix_s):
+    count = win_s.shape[0]
+
+    def some(start, size):
+        windows = [load(win_s, start + i) for i in range(size)]
+        done = attend(windows, gain_ref[...], qkv_ref, proj_ref, bias_s[...], qkv_s, mix_s)
+        for i in range(size):
+            store(win_s, start + i, 0, done[i])
+
+    def step(n, carry):
+        some(n * AT_ONCE, AT_ONCE)
+        return carry
+
+    lax.fori_loop(0, count // AT_ONCE, step, 0)
+    if count % AT_ONCE:
+        some(count - count % AT_ONCE, count % AT_ONCE)
 
 
 def put(win_s, group, start, value):
@@ -174,14 +207,7 @@
 
     bias_s[...] = make_bias(labels_ref, first_row)
 
-    def window(w, carry):
-        done = attend(
-            load(win_s, w), gain_ref[...], qkv_ref, proj_ref, bias_s[...], qkv_s, mix_s
-        )
-        store(win_s, w, 0, done)
-        return carry
-
-    lax.fori_loop(0, win_s.shape[0], window, 0)
+    attend_all(win_s, gain_ref, qkv_ref, proj_ref, bias_s, qkv_s, mix_s)
 
     groups = win_s.shape[1]
     for l in range(LEVELS):
@@ -255,15 +281,19 @@
                 start = (r * levels + l) * WIN_COLS
                 win_s[w, start : start + WIN_COLS, :] = rows[r][l, w * WIN_COLS : (w + 1) * WIN_COLS]
 
-    def window(w, carry):
-        done = attend(win_s[w], gain_ref[...], qkv_ref, proj_ref, None, qkv_s, mix_s)
-        win_s[w] = done
-        spread_s[w] = jnp.dot(
-            norm(done, sgain_ref[...]), sweight_ref[...], preferred_element_type=jnp.float32
-        )
+    count = qkv_s.shape[0]
+
+    def step(n, carry):
+        windows = [win_s[n * count + i] for i in range(count)]
+        done = attend(windows, gain_ref[...], qkv_ref, proj_ref, None, qkv_s, mix_s)
+        for i in range(count):
+            win_s[n * count + i] = done[i]
+            spread_s[n * count + i] = jnp.dot(
+                norm(done[i], sgain_ref[...]), sweight_ref[...], preferred_element_type=jnp.float32
+            )
         return carry
 
-    lax.fori_loop(0, win_s.shape[0], window, 0)
+    lax.fori_loop(0, win_s.shape[0] // count, step, 0)
 
     def gathered(ref, r):
         return jnp.stack(
@@ -355,14 +385,7 @@
 
     bias_s[...] = make_bias(labels_ref, first_row)
 
-    def window(w, carry):
-        done = attend(
-            load(win_s, w), gain_ref[...], qkv_ref, proj_ref, bias_s[...], qkv_s, mix_s
-        )
-        store(win_s, w, 0, done)
-        return carry
-
-    lax.fori_loop(0, win_s.shape[0], window, 0)
+    attend_all(win_s, gain_ref, qkv_ref, proj_ref, bias_s, qkv_s, mix_s)
 
     def natural(l, r):
         base = (l * WIN_ROWS + r) * WIN_COLS
@@ -396,6 +419,10 @@
 
 def bf16(*shape):
     return jax.ShapeDtypeStruct(shape, jnp.bfloat16)
+
+
+def lasting(micros):
+    return pl.CostEstimate(flops=0, bytes_accessed=int(micros * 3.69e6), transcendentals=0)
 
 
 SMEM = pl.BlockSpec(memory_space=pltpu.SMEM)
@@ -414,10 +441,11 @@
         out_specs=(VMEM, VMEM, VMEM),
         scratch_shapes=[
             pltpu.VMEM((count, width // LANES, TOKENS, LANES), jnp.float32),
-            pltpu.VMEM((TOKENS, 3 * width), jnp.bfloat16),
-            pltpu.VMEM((TOKENS, width), jnp.bfloat16),
+            pltpu.VMEM((AT_ONCE, TOKENS, 3 * width), jnp.bfloat16),
+            pltpu.VMEM((AT_ONCE, TOKENS, width), jnp.bfloat16),
             pltpu.VMEM((TOKENS, TOKENS), jnp.float32),
         ],
+        cost_estimate=lasting(13),
         compiler_params=PARAMS,
     )(place, labels, x, lon, main, second, gain, qkv, proj, mgain, mweight)
 
@@ -439,9 +467,10 @@
         scratch_shapes=[
             pltpu.VMEM((count, TOKENS, width), jnp.float32),
             pltpu.VMEM((count, TOKENS, 2 * width), jnp.float32),
-            pltpu.VMEM((TOKENS, 3 * width), jnp.bfloat16),
-            pltpu.VMEM((TOKENS, width), jnp.bfloat16),
+            pltpu.VMEM((math.gcd(count, AT_ONCE), TOKENS, 3 * width), jnp.bfloat16),
+            pltpu.VMEM((math.gcd(count, AT_ONCE), TOKENS, width), jnp.bfloat16),
         ],
+        cost_estimate=lasting(18),
         compiler_params=PARAMS,
     )(first, upper, lower, prev, following, mgain, mweight, gain, qkv, proj, sgain, sweight)
 
@@ -453,6 +482,7 @@
         out_shape=(bf16(*first.shape), bf16(rows, levels, HALF_COLS // 2, width)),
         in_specs=[VMEM] * 5,
         out_specs=(VMEM,) * 2,
+        cost_estimate=lasting(4),
         compiler_params=PARAMS,
     )(first, prev, following, sgain, sweight)
 
@@ -473,11 +503,12 @@
         out_specs=(VMEM,) * 3,
         scratch_shapes=[
             pltpu.VMEM((count, width // LANES, TOKENS, LANES), jnp.float32),
-            pltpu.VMEM((TOKENS, 3 * width), jnp.bfloat16),
-            pltpu.VMEM((TOKENS, width), jnp.bfloat16),
+            pltpu.VMEM((AT_ONCE, TOKENS, 3 * width), jnp.bfloat16),
+            pltpu.VMEM((AT_ONCE, TOKENS, width), jnp.bfloat16),
             pltpu.VMEM((TOKENS, TOKENS), jnp.float32),
             pltpu.VMEM((width // LANES, half, LANES), jnp.float32),
         ],
+        cost_estimate=lasting(9),
         compiler_params=PARAMS,
     )(place, labels, joined, edge, gain, qkv, proj)
 
@@ -535,6 +566,7 @@
         jnp.where(odd, next_second, prev_second), lambda is_odd: (1, -1) if is_odd else (-1, 0)
     )
 
+    x_main, c_second = lax.optimization_barrier((x_main, c_second))
     weights = (flat(gain_first), qkv_first, proj_first, flat(merge_gain), merge_weight)
     first_x, upper_x, lower_x = call_first(
         False, half, place, band_labels, latent, lon, x_main, x_second, *weights
@@ -565,6 +597,7 @@
     own_c, main_c, second_c = call_last(True, place, band_labels, joined_c, edge_c, *weights)
     main_c = send(main_c, lambda is_odd: (1, 0) if is_odd else (-1, 0))
     second_c = send(second_c, lambda is_odd: (1, 0) if is_odd else (-1, 1))
+    own_c, first_x = lax.optimization_barrier((own_c, first_x))
     joined_x, edge_x = call_giver(first_x, back_prev, back_next, flat(split_gain), split_weight)
     edge_x = send(edge_x, lambda is_odd: (-1, 1) if is_odd else (1, 0))
     own_x, main_x, second_x = call_last(False, place, band_labels, joined_x, edge_x, *weights)

time: 163 us -> 130 us (0.80)
  Pallas kernels: 74.7 us -> 43.3 us
  waiting for transfers between devices: 54 us -> 41.2 us
  starting transfers between devices: 22.6 us -> 32.1 us
  local copies, waits for them, and re-layouts: 5.26 us -> 8.32 us
    ppermute x16, waiting for transfers between devices: 54 us -> 41.2 us  [send(): return lax.ppermute(value, ('lat', 'lon'), pairs)]
    pallas_call x2, Pallas kernels: 30.5 us -> 19.1 us  [call_first(): pl.pallas_call(functools.partial(first_kernel, center, half), out_shape=(...]
    ppermute x16, starting transfers between devices: 22.6 us -> 32.1 us  [send(): return lax.ppermute(value, ('lat', 'lon'), pairs)]
    pallas_call x1, Pallas kernels: 19.7 us -> 10.8 us  [call_coarse(): pl.pallas_call(coarse_kernel, out_shape=(bf16(rows, *paired), bf16(2, *pa...]
    pallas_call x2, Pallas kernels: 19.8 us -> 12.4 us  [call_last(): pl.pallas_call(functools.partial(last_kernel, center), out_shape=(bf16(le...]
    pallas_call x1, Pallas kernels: 4.66 us -> 1.04 us  [call_giver(): pl.pallas_call(giver_kernel, out_shape=(bf16(*first.shape), bf16(rows, le...]
    unnamed x22 -> x38, local copies, waits for them, and re-layouts: 5.24 us -> 8.3 us
  transfers between devices with their start and end apart: 16 -> 16, of which waited for: 6 -> 6; matrix products, arithmetic and copies ran while one was open for 2% -> 1% of each run, Pallas kernels for 34% -> 24%
where the time goes in v2:
time: 130 us
  Pallas kernels  43.3 us (33%)
  waiting for transfers between devices  41.2 us (32%)
  starting transfers between devices  32.1 us (25%)
  local copies, waits for them, and re-layouts  8.32 us (6%)
  other arithmetic  4.66 us (4%)
    ppermute x16, waiting for transfers between devices, send(): return lax.ppermute(value, ('lat', 'lon'), pairs)  41.2 us
    ppermute x16, starting transfers between devices, send(): return lax.ppermute(value, ('lat', 'lon'), pairs)  32.1 us
    pallas_call x2, Pallas kernels, call_first(): pl.pallas_call(functools.partial(first_kernel, center, half), out_shape=(...  19.1 us
    pallas_call x2, Pallas kernels, call_last(): pl.pallas_call(functools.partial(last_kernel, center), out_shape=(bf16(le...  12.4 us
    pallas_call x1, Pallas kernels, call_coarse(): pl.pallas_call(coarse_kernel, out_shape=(bf16(rows, *paired), bf16(2, *pa...  10.8 us
    unnamed x38, local copies, waits for them, and re-layouts  8.3 us
  transfers between devices with their start and end apart: 16, of which 6 were waited for; matrix products, arithmetic and copies ran while one was open for 1% of the time, Pallas kernels for 24%

profile of v2, /device:TPU:0, one launch (start us, length us, event | category | flops | bytes accessed | tf_op | source)
XLA Modules:
  0.0 129.7 jit_solution(10297770639586532269)
XLA Ops:
  0.0 1.5 %broadcast_select_fusion.2 = (bf16[3,3,42,512]{3,2,1,0:T(8,128)(2,1)S(1)}, bf16[3,3,42,512]{3,2,1,0:T(8,128)(2,1)S(1)}) fusion(pred[]{:T(512)S(6)} %eq.5, bf16[3,6,96,512]{3,2,1,0:T(8,128)(2,1)} %x_ref.3), kind=kLoop, calls=%fused_computation.3 | loop fusion | flops 387072 | bytes 1548289 | tf_op jit(solution)/shard_map/jit(_where)/select_n | solution.py:560
  1.5 3.1 %collective-permute-start.2 = (bf16[3,3,42,512]{3,2,1,0:T(8,128)(2,1)S(1)}, bf16[3,3,42,512]{3,2,1,0:T(8,128)(2,1)S(1)}, u32[]{:S(2)}, u32[]{:S(2)}) collective-permute-start(bf16[3,3,42,512]{3,2,1,0:T(8,128)(2,1)S(1)} %get-tuple-element.52), channel_id=1, source_target_pairs={{0,8},{2,10},{4,12},{6,14},{8,0},{10,2},{12,4},{14,6},{16,24},{18,... | collective-permute-start | bytes 1161224 | tf_op jit(solution)/shard_map/ppermute | solution.py:524
  4.6 1.2 broadcast_select_fusion.6
  5.9 2.5 %collective-permute-start.3 = (bf16[3,3,18,512]{3,2,1,0:T(8,128)(2,1)S(1)}, bf16[3,3,18,512]{3,2,1,0:T(8,128)(2,1)S(1)}, u32[]{:S(2)}, u32[]{:S(2)}) collective-permute-start(bf16[3,3,18,512]{3,2,1,0:T(8,128)(2,1)S(1)} %get-tuple-element.51), channel_id=1, source_target_pairs={{0,24},{2,26},{4,28},{6,30},{8,22},{10,16},{12,18},{14,20},{16,8},... | collective-permute-start | bytes 497672 | tf_op jit(solution)/shard_map/ppermute | solution.py:524
  8.4 1.3 %collective-permute-start.4 = (bf16[3,3,18,512]{3,2,1,0:T(8,128)(2,1)S(1)}, bf16[3,3,18,512]{3,2,1,0:T(8,128)(2,1)S(1)}, u32[]{:S(2)}, u32[]{:S(2)}) collective-permute-start(bf16[3,3,18,512]{3,2,1,0:T(8,128)(2,1)S(1)} %get-tuple-element.49), channel_id=1, source_target_pairs={{0,14},{2,8},{4,10},{6,12},{8,0},{10,2},{12,4},{14,6},{16,30},{18,... | collective-permute-start | bytes 497672 | tf_op jit(solution)/shard_map/ppermute | solution.py:524
  9.7 1.2 collective-permute-start.1
  11.0 9.8 %collective-permute-done.3.second_ref = bf16[3,3,18,512]{3,2,1,0:T(8,128)(2,1)S(1)} collective-permute-done((bf16[3,3,18,512]{3,2,1,0:T(8,128)(2,1)S(1)}, bf16[3,3,18,512]{3,2,1,0:T(8,128)(2,1)S(1)}, u32[]{:S(2)}, u32[]{:S(2)}) %collective-permute-start.3) | collective-permute-done | bytes 165920 | tf_op jit(solution)/shard_map/ppermute | solution.py:524
  20.7 4.0 %collective-permute-done.4.second_ref = bf16[3,3,18,512]{3,2,1,0:T(8,128)(2,1)S(1)} collective-permute-done((bf16[3,3,18,512]{3,2,1,0:T(8,128)(2,1)S(1)}, bf16[3,3,18,512]{3,2,1,0:T(8,128)(2,1)S(1)}, u32[]{:S(2)}, u32[]{:S(2)}) %collective-permute-start.4) | collective-permute-done | bytes 165920 | tf_op jit(solution)/shard_map/ppermute | solution.py:524
  24.7 2.2 %copy-done = bf16[2048,1024]{1,0:T(8,128)(2,1)S(1)} copy-done((bf16[2048,1024]{1,0:T(8,128)(2,1)S(1)}, bf16[2048,1024]{1,0:T(8,128)(2,1)}, u32[]{:S(2)}) %copy-start) | copy-done | bytes 4194328
  26.9 1.4 %copy-done.4 = bf16[512,1536]{1,0:T(8,128)(2,1)S(1)} copy-done((bf16[512,1536]{1,0:T(8,128)(2,1)S(1)}, bf16[512,1536]{1,0:T(8,128)(2,1)}, u32[]{:S(2)}) %copy-start.4) | copy-done | bytes 1572888
  28.3 1.0 copy-done.8
  29.4 0.7 copy-done.11
  30.1 0.7 copy-done.14
  30.8 0.7 copy-done.17
  31.4 9.5 %shard_map.146 = (bf16[6,3,24,1024]{3,2,1,0:T(8,128)(2,1)S(1)}, bf16[2,3,24,1024]{3,2,1,0:T(8,128)(2,1)S(1)}, bf16[2,3,24,1024]{3,2,1,0:T(8,128)(2,1)S(1)}) custom-call(s32[1]{0:T(128)} %bitcast.place_ref, s32[24]{0:T(128)S(1)} %copy-done.17, bf16[3,6,96,512]{3,2,1,0:T(8,128)(2,1)S(1)} %copy-done.3, ...), custom_call_target="tpu_custom_call" | custom-call | bytes 47970000 | tf_op jit(solution)/shard_map/pallas_call | solution.py:437
  41.2 3.6 %collective-permute-start.6 = (bf16[2,3,24,1024]{3,2,1,0:T(8,128)(2,1)S(1)}, bf16[2,3,24,1024]{3,2,1,0:T(8,128)(2,1)S(1)}, u32[]{:S(2)}, u32[]{:S(2)}) collective-permute-start(bf16[2,3,24,1024]{3,2,1,0:T(8,128)(2,1)S(1)} %get-tuple-element.33), channel_id=1, source_target_pairs={{0,24},{2,26},{4,28},{6,30},{8,0},{10,2},{12,4},{14,6},{16,8},{18,... | collective-permute-start | bytes 884744 | tf_op jit(solution)/shard_map/ppermute | solution.py:524
  44.8 9.6 %shard_map.145 = (bf16[6,3,24,1024]{3,2,1,0:T(8,128)(2,1)S(1)}, bf16[2,3,24,1024]{3,2,1,0:T(8,128)(2,1)S(1)}, bf16[2,3,24,1024]{3,2,1,0:T(8,128)(2,1)S(1)}) custom-call(s32[1]{0:T(128)} %bitcast.place_ref, s32[24]{0:T(128)S(1)} %copy-done.17, bf16[3,6,96,512]{3,2,1,0:T(8,128)(2,1)S(1)} %copy-done.3, ...), custom_call_target="tpu_custom_call" | custom-call | bytes 47970000 | tf_op jit(solution)/shard_map/pallas_call | solution.py:437
  54.4 4.5 %collective-permute-done.6.next_ref = bf16[2,3,24,1024]{3,2,1,0:T(8,128)(2,1)S(1)} collective-permute-done((bf16[2,3,24,1024]{3,2,1,0:T(8,128)(2,1)S(1)}, bf16[2,3,24,1024]{3,2,1,0:T(8,128)(2,1)S(1)}, u32[]{:S(2)}, u32[]{:S(2)}) %collective-permute-start.6) | collective-permute-done | bytes 294944 | tf_op jit(solution)/shard_map/ppermute | solution.py:524
  59.0 1.6 %copy-done.10 = bf16[1024,1024]{1,0:T(8,128)(2,1)S(1)} copy-done((bf16[1024,1024]{1,0:T(8,128)(2,1)S(1)}, bf16[1024,1024]{1,0:T(8,128)(2,1)}, u32[]{:S(2)}) %copy-start.10) | copy-done | bytes 2097176
  60.6 10.8 %shard_map.147 = (bf16[6,3,24,1024]{3,2,1,0:T(8,128)(2,1)S(1)}, bf16[2,3,24,1024]{3,2,1,0:T(8,128)(2,1)S(1)}, bf16[2,3,24,1024]{3,2,1,0:T(8,128)(2,1)S(1)}, bf16[6,3,3,1024]{3,2,1,0:T(4,128)(2,1)S(1)}) custom-call(bf16[6,3,24,1024]{3,2,1,0:T(8,128)(2,1)S(1)} %get-tuple-element.28.first_ref, bf16[2,3,24,1024]{3,2,1,0:T(8,128)(2,1)S(1)} %get-tuple-element.29.upper_ref, ...), custom_call_target="tpu_custom_call" | custom-call | bytes 66420000 | tf_op jit(solution)/shard_map/pallas_call | solution.py:457
  71.4 3.8 %collective-permute-start.9 = (bf16[2,3,24,1024]{3,2,1,0:T(8,128)(2,1)S(1)}, bf16[2,3,24,1024]{3,2,1,0:T(8,128)(2,1)S(1)}, u32[]{:S(2)}, u32[]{:S(2)}) collective-permute-start(bf16[2,3,24,1024]{3,2,1,0:T(8,128)(2,1)S(1)} %get-tuple-element.40), channel_id=1, source_target_pairs={{0,24},{2,26},{4,28},{6,30},{8,0},{10,2},{12,4},{14,6},{16,8},{18,... | collective-permute-start | bytes 884744 | tf_op jit(solution)/shard_map/ppermute | solution.py:524
  75.3 4.4 %collective-permute-start.7 = (bf16[6,3,3,1024]{3,2,1,0:T(4,128)(2,1)S(1)}, bf16[6,3,3,1024]{3,2,1,0:T(4,128)(2,1)S(1)}, u32[]{:S(2)}, u32[]{:S(2)}) collective-permute-start(bf16[6,3,3,1024]{3,2,1,0:T(4,128)(2,1)S(1)} %get-tuple-element.35), channel_id=1, source_target_pairs={{0,26},{2,28},{4,30},{6,24},{8,16},{10,18},{12,20},{14,22},{16,10}... | collective-permute-start | bytes 331784 | tf_op jit(solution)/shard_map/ppermute | solution.py:524
  79.6 9.0 %collective-permute-done.7.edge_ref = bf16[6,3,3,1024]{3,2,1,0:T(4,128)(2,1)S(1)} collective-permute-done((bf16[6,3,3,1024]{3,2,1,0:T(4,128)(2,1)S(1)}, bf16[6,3,3,1024]{3,2,1,0:T(4,128)(2,1)S(1)}, u32[]{:S(2)}, u32[]{:S(2)}) %collective-permute-start.7) | collective-permute-done | bytes 110624 | tf_op jit(solution)/shard_map/ppermute | solution.py:524
  88.6 6.2 %shard_map.148 = (bf16[3,3,48,512]{3,2,1,0:T(8,128)(2,1)S(1)}, bf16[3,3,42,512]{3,2,1,0:T(8,128)(2,1)S(1)}, bf16[3,3,6,512]{3,2,1,0:T(8,128)(2,1)S(1)}) custom-call(s32[1]{0:T(128)} %bitcast.place_ref, s32[24]{0:T(128)S(1)} %copy-done.17, bf16[6,3,24,1024]{3,2,1,0:T(8,128)(2,1)S(1)} %get-tuple-element.34.joined_ref, ...), custom_call_target="tpu_custom_call" | custom-call | bytes 33210000 | tf_op jit(solution)/shard_map/pallas_call | solution.py:495
  94.8 1.0 shard_map.149
  95.9 5.2 %collective-permute-start.10 = (bf16[6,3,3,1024]{3,2,1,0:T(4,128)(2,1)S(1)}, bf16[6,3,3,1024]{3,2,1,0:T(4,128)(2,1)S(1)}, u32[]{:S(2)}, u32[]{:S(2)}) collective-permute-start(bf16[6,3,3,1024]{3,2,1,0:T(4,128)(2,1)S(1)} %get-tuple-element.42), channel_id=1, source_target_pairs={{0,8},{2,10},{4,12},{6,14},{8,2},{10,4},{12,6},{14,0},{16,24},{18,... | collective-permute-start | bytes 331784 | tf_op jit(solution)/shard_map/ppermute | solution.py:524
  101.1 3.8 %collective-permute-start.13 = (bf16[3,3,42,512]{3,2,1,0:T(8,128)(2,1)S(1)}, bf16[3,3,42,512]{3,2,1,0:T(8,128)(2,1)S(1)}, u32[]{:S(2)}, u32[]{:S(2)}) collective-permute-start(bf16[3,3,42,512]{3,2,1,0:T(8,128)(2,1)S(1)} %get-tuple-element.46), channel_id=1, source_target_pairs={{0,24},{2,26},{4,28},{6,30},{8,16},{10,18},{12,20},{14,22},{16,8},... | collective-permute-start | bytes 1161224 | tf_op jit(solution)/shard_map/ppermute | solution.py:524
  104.9 6.2 %shard_map.150 = (bf16[3,3,48,512]{3,2,1,0:T(8,128)(2,1)S(1)}, bf16[3,3,42,512]{3,2,1,0:T(8,128)(2,1)S(1)}, bf16[3,3,6,512]{3,2,1,0:T(8,128)(2,1)S(1)}) custom-call(s32[1]{0:T(128)} %bitcast.place_ref, s32[24]{0:T(128)S(1)} %copy-done.17, bf16[6,3,24,1024]{3,2,1,0:T(8,128)(2,1)S(1)} %get-tuple-element.41.joined_ref, ...), custom_call_target="tpu_custom_call" | custom-call | bytes 33210000 | tf_op jit(solution)/shard_map/pallas_call | solution.py:495
  111.1 2.5 %collective-permute-start.14 = (bf16[3,3,6,512]{3,2,1,0:T(8,128)(2,1)S(1)}, bf16[3,3,6,512]{3,2,1,0:T(8,128)(2,1)S(1)}, u32[]{:S(2)}, u32[]{:S(2)}) collective-permute-start(bf16[3,3,6,512]{3,2,1,0:T(8,128)(2,1)S(1)} %get-tuple-element.47), channel_id=1, source_target_pairs={{0,8},{2,10},{4,12},{6,14},{8,2},{10,4},{12,6},{14,0},{16,24},{18,... | collective-permute-start | bytes 165896 | tf_op jit(solution)/shard_map/ppermute | solution.py:524
  113.9 5.1 %collective-permute-done.14 = bf16[3,3,6,512]{3,2,1,0:T(8,128)(2,1)S(1)} collective-permute-done((bf16[3,3,6,512]{3,2,1,0:T(8,128)(2,1)S(1)}, bf16[3,3,6,512]{3,2,1,0:T(8,128)(2,1)S(1)}, u32[]{:S(2)}, u32[]{:S(2)}) %collective-permute-start.14) | collective-permute-done | bytes 55328 | tf_op jit(solution)/shard_map/ppermute | solution.py:524
  119.1 8.8 %collective-permute-done.12 = bf16[3,3,42,512]{3,2,1,0:T(8,128)(2,1)S(1)} collective-permute-done((bf16[3,3,42,512]{3,2,1,0:T(8,128)(2,1)S(1)}, bf16[3,3,42,512]{3,2,1,0:T(8,128)(2,1)S(1)}, u32[]{:S(2)}, u32[]{:S(2)}) %collective-permute-start.12) | collective-permute-done | bytes 387104 | tf_op jit(solution)/shard_map/ppermute | solution.py:524
  127.9 1.8 %maximum_maximum_fusion = bf16[3,6,96,512]{3,2,1,0:T(8,128)(2,1)} fusion(bf16[3,3,42,512]{3,2,1,0:T(8,128)(2,1)S(1)} %get-tuple-element.55, bf16[3,3,48,512]{3,2,1,0:T(8,128)(2,1)S(1)} %get-tuple-element.57, bf16[3,3,6,512]{3,2,1,0:T(8,128)(2,1)S(1)} %get-tuple-element.59, bf16[3,3,42,512]{3,2,1,0:T(8,128)(2,1)S(1)} %bitcast.17, ...), kind=kLoop, calls=%fused_computation | loop fusion | flops 12386304 | bytes 3538944 | tf_op jit(solution)/shard_map/concatenate | solution.py:614
  (51 shorter events, 0.7 us)
Async XLA Ops:
  0.0 24.7 %copy-start.3 = (bf16[3,6,96,512]{3,2,1,0:T(8,128)(2,1)S(1)}, bf16[3,6,96,512]{3,2,1,0:T(8,128)(2,1)}, u32[]{:S(2)}) copy-start(bf16[3,6,96,512]{3,2,1,0:T(8,128)(2,1)} %x_ref.3) | copy-start | bytes 5308420
  1.5 19.2 %collective-permute-start.2 = (bf16[3,3,42,512]{3,2,1,0:T(8,128)(2,1)S(1)}, bf16[3,3,42,512]{3,2,1,0:T(8,128)(2,1)S(1)}, u32[]{:S(2)}, u32[]{:S(2)}) collective-permute-start(bf16[3,3,42,512]{3,2,1,0:T(8,128)(2,1)S(1)} %get-tuple-element.52), channel_id=1, source_target_pairs={{0,8},{2,10},{4,12},{6,14},{8,0},{10,2},{12,4},{14,6},{16,24},{18,... | collective-permute-start | bytes 1161224 | tf_op jit(solution)/shard_map/ppermute | solution.py:524
  4.6 40.2 %copy-start.12 = (f32[2048]{0:T(1024)S(1)}, f32[2048]{0:T(1024)}, u32[]{:S(2)}) copy-start(f32[2048]{0:T(1024)} %param.20) | copy-start | bytes 24580
  4.6 40.2 %copy-start.15 = (f32[512]{0:T(512)S(1)}, f32[512]{0:T(512)}, u32[]{:S(2)}) copy-start(f32[512]{0:T(512)} %param.17) | copy-start | bytes 6148
  5.9 14.9 %collective-permute-start.3 = (bf16[3,3,18,512]{3,2,1,0:T(8,128)(2,1)S(1)}, bf16[3,3,18,512]{3,2,1,0:T(8,128)(2,1)S(1)}, u32[]{:S(2)}, u32[]{:S(2)}) collective-permute-start(bf16[3,3,18,512]{3,2,1,0:T(8,128)(2,1)S(1)} %get-tuple-element.51), channel_id=1, source_target_pairs={{0,24},{2,26},{4,28},{6,30},{8,22},{10,16},{12,18},{14,20},{16,8},... | collective-permute-start | bytes 497672 | tf_op jit(solution)/shard_map/ppermute | solution.py:524
  8.4 16.3 %collective-permute-start.4 = (bf16[3,3,18,512]{3,2,1,0:T(8,128)(2,1)S(1)}, bf16[3,3,18,512]{3,2,1,0:T(8,128)(2,1)S(1)}, u32[]{:S(2)}, u32[]{:S(2)}) collective-permute-start(bf16[3,3,18,512]{3,2,1,0:T(8,128)(2,1)S(1)} %get-tuple-element.49), channel_id=1, source_target_pairs={{0,14},{2,8},{4,10},{6,12},{8,0},{10,2},{12,4},{14,6},{16,30},{18,... | collective-permute-start | bytes 497672 | tf_op jit(solution)/shard_map/ppermute | solution.py:524
  9.7 15.0 %collective-permute-start = (bf16[3,3,18,512]{3,2,1,0:T(8,128)(2,1)S(1)}, bf16[3,3,18,512]{3,2,1,0:T(8,128)(2,1)S(1)}, u32[]{:S(2)}, u32[]{:S(2)}) collective-permute-start(bf16[3,3,18,512]{3,2,1,0:T(8,128)(2,1)S(1)} %get-tuple-element.50), channel_id=1, source_target_pairs={{0,6},{2,0},{4,2},{6,4},{8,14},{10,8},{12,10},{14,12},{16,22},{18,... | collective-permute-start | bytes 497672 | tf_op jit(solution)/shard_map/ppermute | solution.py:524
  9.7 35.1 %collective-permute-start.1 = (bf16[3,3,42,512]{3,2,1,0:T(8,128)(2,1)S(1)}, bf16[3,3,42,512]{3,2,1,0:T(8,128)(2,1)S(1)}, u32[]{:S(2)}, u32[]{:S(2)}) collective-permute-start(bf16[3,3,42,512]{3,2,1,0:T(8,128)(2,1)S(1)} %get-tuple-element.53), channel_id=1, source_target_pairs={{0,24},{2,26},{4,28},{6,30},{8,16},{10,18},{12,20},{14,22},{16,8},... | collective-permute-start | bytes 1161224 | tf_op jit(solution)/shard_map/ppermute | solution.py:524
  24.7 2.2 %copy-start = (bf16[2048,1024]{1,0:T(8,128)(2,1)S(1)}, bf16[2048,1024]{1,0:T(8,128)(2,1)}, u32[]{:S(2)}) copy-start(bf16[2048,1024]{1,0:T(8,128)(2,1)} %mweight_ref.5) | copy-start | bytes 12582916
  26.9 1.4 %copy-start.4 = (bf16[512,1536]{1,0:T(8,128)(2,1)S(1)}, bf16[512,1536]{1,0:T(8,128)(2,1)}, u32[]{:S(2)}) copy-start(bf16[512,1536]{1,0:T(8,128)(2,1)} %qkv_ref.6) | copy-start | bytes 4718596
  28.3 1.0 copy-start.8
  31.4 13.4 %copy-start.1 = (bf16[2048,1024]{1,0:T(8,128)(2,1)S(1)}, bf16[2048,1024]{1,0:T(8,128)(2,1)}, u32[]{:S(2)}) copy-start(bf16[2048,1024]{1,0:T(8,128)(2,1)} %mweight_ref.5) | copy-start | bytes 12582916
  31.4 13.4 %copy-start.5 = (bf16[512,1536]{1,0:T(8,128)(2,1)S(1)}, bf16[512,1536]{1,0:T(8,128)(2,1)}, u32[]{:S(2)}) copy-start(bf16[512,1536]{1,0:T(8,128)(2,1)} %qkv_ref.6) | copy-start | bytes 4718596
  31.4 27.6 %copy-start.7 = (bf16[1024,3072]{1,0:T(8,128)(2,1)S(1)}, bf16[1024,3072]{1,0:T(8,128)(2,1)}, u32[]{:S(2)}) copy-start(bf16[1024,3072]{1,0:T(8,128)(2,1)} %qkv_ref.7) | copy-start | bytes 18874372
  40.9 13.5 %collective-permute-start.5 = (bf16[2,3,24,1024]{3,2,1,0:T(8,128)(2,1)S(1)}, bf16[2,3,24,1024]{3,2,1,0:T(8,128)(2,1)S(1)}, u32[]{:S(2)}, u32[]{:S(2)}) collective-permute-start(bf16[2,3,24,1024]{3,2,1,0:T(8,128)(2,1)S(1)} %get-tuple-element.32), channel_id=1, source_target_pairs={{0,8},{2,10},{4,12},{6,14},{8,16},{10,18},{12,20},{14,22},{16,24},... | collective-permute-start | bytes 884744 | tf_op jit(solution)/shard_map/ppermute | solution.py:524
  41.2 17.8 %copy-start.2 = (bf16[1024,2048]{1,0:T(8,128)(2,1)S(1)}, bf16[1024,2048]{1,0:T(8,128)(2,1)}, u32[]{:S(2)}) copy-start(bf16[1024,2048]{1,0:T(8,128)(2,1)} %sweight_ref.3) | copy-start | bytes 12582916
  41.2 17.8 %copy-start.13 = (f32[1024]{0:T(1024)S(1)}, f32[1024]{0:T(1024)}, u32[]{:S(2)}) copy-start(f32[1024]{0:T(1024)} %param.25) | copy-start | bytes 12292
  41.2 17.8 %copy-start.18 = (f32[1024]{0:T(1024)S(1)}, f32[1024]{0:T(1024)}, u32[]{:S(2)}) copy-start(f32[1024]{0:T(1024)} %param.22) | copy-start | bytes 12292
  41.2 17.8 %collective-permute-start.6 = (bf16[2,3,24,1024]{3,2,1,0:T(8,128)(2,1)S(1)}, bf16[2,3,24,1024]{3,2,1,0:T(8,128)(2,1)S(1)}, u32[]{:S(2)}, u32[]{:S(2)}) collective-permute-start(bf16[2,3,24,1024]{3,2,1,0:T(8,128)(2,1)S(1)} %get-tuple-element.33), channel_id=1, source_target_pairs={{0,24},{2,26},{4,28},{6,30},{8,0},{10,2},{12,4},{14,6},{16,8},{18,... | collective-permute-start | bytes 884744 | tf_op jit(solution)/shard_map/ppermute | solution.py:524
  59.0 1.6 %copy-start.10 = (bf16[1024,1024]{1,0:T(8,128)(2,1)S(1)}, bf16[1024,1024]{1,0:T(8,128)(2,1)}, u32[]{:S(2)}) copy-start(bf16[1024,1024]{1,0:T(8,128)(2,1)} %proj_ref.7) | copy-start | bytes 6291460
  60.6 28.0 %copy-start.6 = (bf16[512,1536]{1,0:T(8,128)(2,1)S(1)}, bf16[512,1536]{1,0:T(8,128)(2,1)}, u32[]{:S(2)}) copy-start(bf16[512,1536]{1,0:T(8,128)(2,1)} %qkv_ref.9) | copy-start | bytes 4718596
  60.6 28.0 %copy-start.9 = (bf16[512,512]{1,0:T(8,128)(2,1)S(1)}, bf16[512,512]{1,0:T(8,128)(2,1)}, u32[]{:S(2)}) copy-start(bf16[512,512]{1,0:T(8,128)(2,1)} %proj_ref.9) | copy-start | bytes 1572868
  60.6 28.0 %copy-start.16 = (f32[512]{0:T(512)S(1)}, f32[512]{0:T(512)}, u32[]{:S(2)}) copy-start(f32[512]{0:T(512)} %param.27) | copy-start | bytes 6148
  71.4 23.4 %collective-permute-start.8 = (bf16[2,3,24,1024]{3,2,1,0:T(8,128)(2,1)S(1)}, bf16[2,3,24,1024]{3,2,1,0:T(8,128)(2,1)S(1)}, u32[]{:S(2)}, u32[]{:S(2)}) collective-permute-start(bf16[2,3,24,1024]{3,2,1,0:T(8,128)(2,1)S(1)} %get-tuple-element.39), channel_id=1, source_target_pairs={{0,8},{2,10},{4,12},{6,14},{8,16},{10,18},{12,20},{14,22},{16,24},... | collective-permute-start | bytes 884744 | tf_op jit(solution)/shard_map/ppermute | solution.py:524
  71.4 23.4 %collective-permute-start.9 = (bf16[2,3,24,1024]{3,2,1,0:T(8,128)(2,1)S(1)}, bf16[2,3,24,1024]{3,2,1,0:T(8,128)(2,1)S(1)}, u32[]{:S(2)}, u32[]{:S(2)}) collective-permute-start(bf16[2,3,24,1024]{3,2,1,0:T(8,128)(2,1)S(1)} %get-tuple-element.40), channel_id=1, source_target_pairs={{0,24},{2,26},{4,28},{6,30},{8,0},{10,2},{12,4},{14,6},{16,8},{18,... | collective-permute-start | bytes 884744 | tf_op jit(solution)/shard_map/ppermute | solution.py:524
  75.3 13.4 %collective-permute-start.7 = (bf16[6,3,3,1024]{3,2,1,0:T(4,128)(2,1)S(1)}, bf16[6,3,3,1024]{3,2,1,0:T(4,128)(2,1)S(1)}, u32[]{:S(2)}, u32[]{:S(2)}) collective-permute-start(bf16[6,3,3,1024]{3,2,1,0:T(4,128)(2,1)S(1)} %get-tuple-element.35), channel_id=1, source_target_pairs={{0,26},{2,28},{4,30},{6,24},{8,16},{10,18},{12,20},{14,22},{16,10}... | collective-permute-start | bytes 331784 | tf_op jit(solution)/shard_map/ppermute | solution.py:524
  95.9 9.0 %collective-permute-start.10 = (bf16[6,3,3,1024]{3,2,1,0:T(4,128)(2,1)S(1)}, bf16[6,3,3,1024]{3,2,1,0:T(4,128)(2,1)S(1)}, u32[]{:S(2)}, u32[]{:S(2)}) collective-permute-start(bf16[6,3,3,1024]{3,2,1,0:T(4,128)(2,1)S(1)} %get-tuple-element.42), channel_id=1, source_target_pairs={{0,8},{2,10},{4,12},{6,14},{8,2},{10,4},{12,6},{14,0},{16,24},{18,... | collective-permute-start | bytes 331784 | tf_op jit(solution)/shard_map/ppermute | solution.py:524
  101.1 12.9 %collective-permute-start.15 = (bf16[3,3,6,512]{3,2,1,0:T(8,128)(2,1)S(1)}, bf16[3,3,6,512]{3,2,1,0:T(8,128)(2,1)S(1)}, u32[]{:S(2)}, u32[]{:S(2)}) collective-permute-start(bf16[3,3,6,512]{3,2,1,0:T(8,128)(2,1)S(1)} %get-tuple-element.48), channel_id=1, source_target_pairs={{0,26},{2,28},{4,30},{6,24},{8,16},{10,18},{12,20},{14,22},{16,10}... | collective-permute-start | bytes 165896 | tf_op jit(solution)/shard_map/ppermute | solution.py:524
  101.1 18.0 %collective-permute-start.13 = (bf16[3,3,42,512]{3,2,1,0:T(8,128)(2,1)S(1)}, bf16[3,3,42,512]{3,2,1,0:T(8,128)(2,1)S(1)}, u32[]{:S(2)}, u32[]{:S(2)}) collective-permute-start(bf16[3,3,42,512]{3,2,1,0:T(8,128)(2,1)S(1)} %get-tuple-element.46), channel_id=1, source_target_pairs={{0,24},{2,26},{4,28},{6,30},{8,16},{10,18},{12,20},{14,22},{16,8},... | collective-permute-start | bytes 1161224 | tf_op jit(solution)/shard_map/ppermute | solution.py:524
  111.1 7.9 %collective-permute-start.14 = (bf16[3,3,6,512]{3,2,1,0:T(8,128)(2,1)S(1)}, bf16[3,3,6,512]{3,2,1,0:T(8,128)(2,1)S(1)}, u32[]{:S(2)}, u32[]{:S(2)}) collective-permute-start(bf16[3,3,6,512]{3,2,1,0:T(8,128)(2,1)S(1)} %get-tuple-element.47), channel_id=1, source_target_pairs={{0,8},{2,10},{4,12},{6,14},{8,2},{10,4},{12,6},{14,0},{16,24},{18,... | collective-permute-start | bytes 165896 | tf_op jit(solution)/shard_map/ppermute | solution.py:524
  113.6 14.2 %collective-permute-start.12 = (bf16[3,3,42,512]{3,2,1,0:T(8,128)(2,1)S(1)}, bf16[3,3,42,512]{3,2,1,0:T(8,128)(2,1)S(1)}, u32[]{:S(2)}, u32[]{:S(2)}) collective-permute-start(bf16[3,3,42,512]{3,2,1,0:T(8,128)(2,1)S(1)} %get-tuple-element.45), channel_id=1, source_target_pairs={{0,8},{2,10},{4,12},{6,14},{8,0},{10,2},{12,4},{14,6},{16,24},{18,... | collective-permute-start | bytes 1161224 | tf_op jit(solution)/shard_map/ppermute | solution.py:524
  113.8 14.1 %collective-permute-start.11 = (bf16[3,3,6,512]{3,2,1,0:T(8,128)(2,1)S(1)}, bf16[3,3,6,512]{3,2,1,0:T(8,128)(2,1)S(1)}, u32[]{:S(2)}, u32[]{:S(2)}) collective-permute-start(bf16[3,3,6,512]{3,2,1,0:T(8,128)(2,1)S(1)} %slice.35), channel_id=1, source_target_pairs={{0,2},{2,4},{4,6},{6,0},{8,10},{10,12},{12,14},{14,8},{16,18},{18,... | collective-permute-start | bytes 165896 | tf_op jit(solution)/shard_map/ppermute | solution.py:524
  (3 other events, 2.0 us)
